TPU v7x, 128 devices: a whole 4x4x4 slice. The times are simulated.
128 devices in a mesh: dp: 32 (over x, z, core), rep: 4 (over y).
Axes of the slice: x: 4, y: 4, z: 4, core: 2. Of those that a mesh axis runs over, the one named last changes fastest.
Arguments:
- page_pool: bfloat16 [14336, 64, 576], P(('rep', 'dp')), parts along dimension 0, may hold values from -12 to 12
- move_source: int32 [3072, 1], P('rep'), parts along dimension 0, may hold values from 0 to 31; in each aligned block of 24 rows (0 to 23, 24 to 47, ...) at most 2 rows name the same one
- move_page: int32 [3072], P('rep'), parts along dimension 0, may hold values from 0 to 111
- move_slot: int32 [3072], P('rep'), parts along dimension 0, may hold values from 0 to 111, as said below
- row_count: int32 [128], P(('rep', 'dp')), parts along dimension 0, may hold values from 1 to 16, as said below
- lengths: int32 [2048], P(('rep', 'dp')), parts along dimension 0, may hold values from 1 to 2048, as said below
- page_table: int32 [2048, 32], P(('rep', 'dp')), parts along dimension 0, may hold values from 0 to 111
- queries: bfloat16 [2048, 64, 576], P(('rep', 'dp')), parts along dimension 0, may hold values from -32 to 32
- value_up: bfloat16 [64, 512, 128], P('dp'), may hold values from -0.25 to 0.25
- out_proj: bfloat16 [8192, 7168], P('dp'), may hold values from -0.375 to 0.375
- residual: bfloat16 [2048, 7168], P(('rep', 'dp')), parts along dimension 0, may hold values from -6 to 6
- norm_gain: float32 [7168], replicated, may hold values from 0.1 to 1.9
- gate_proj: bfloat16 [7168, 9216], P(None, 'dp'), may hold values from -0.0625 to 0.0625
- up_proj: bfloat16 [7168, 9216], P(None, 'dp'), may hold values from -0.0625 to 0.0625
- down_proj: bfloat16 [9216, 7168], P('dp'), may hold values from -0.0625 to 0.0625
Outputs:
- layer_out: bfloat16 [2048, 7168], P(('rep', 'dp')), parts along dimension 0
There are 4 independent parts, one for each index of `rep`. A program takes and returns all parts, laid end to end along the dimension named above; an argument that names none is the same for every part. Nothing has to cross between parts.
Inputs may be any that keep to these rules, and one draw needn't show every extreme that they name: `move_source`: within the 24 moves of one destination rank, no source rank appears more than 2 times, and some source appears exactly 2 times. `move_slot`: the 24 slots of one destination rank are distinct. `row_count`: some rank has exactly 16 live rows. `lengths`: some row has exactly 2048 tokens.
All inputs are finite; a program needn't handle non-finite values.
Results may differ from a plain program's by a relative error of at most 0.02.
Values may be sent and summed in bfloat16 or wider, within the bound.
A program may use at most 128 MiB of HBM per device.

v0:
```python
import jax
import jax.numpy as jnp
from jax import lax
from jax.sharding import PartitionSpec as P

LATENT = 512


SOFTMAX_SCALE = 192 ** (-0.5)


def rms_scale(values, gain_row):
    factor = lax.rsqrt(jnp.mean(values * values, axis=-1, keepdims=True) + 1e-06)
    return (values * factor * gain_row).astype(jnp.bfloat16)


def attend_rows(cache_pages, tables, row_lens, queries, valid_rows):

    def one_row(inputs):
        table_row, row_len, query_row = inputs
        tokens = cache_pages[table_row].reshape(-1, cache_pages.shape[2])
        scores = (
            jnp.einsum("hk,tk->ht", query_row, tokens, preferred_element_type=jnp.float32)
            * SOFTMAX_SCALE
        )
        live_mask = jnp.arange(tokens.shape[0]) < row_len
        scores = jnp.where(live_mask[None, :], scores, -jnp.inf)
        top_score = jnp.max(scores, axis=1, keepdims=True)
        exponent = jnp.exp(scores - top_score)
        weights = (exponent / jnp.sum(exponent, axis=1, keepdims=True)).astype(jnp.bfloat16)
        return jnp.einsum(
            "ht,tl->hl", weights, tokens[:, :LATENT], preferred_element_type=jnp.float32
        ).astype(jnp.bfloat16)

    outputs = lax.map(one_row, (tables, row_lens, queries))
    return jnp.where(valid_rows[:, None, None], outputs, jnp.zeros_like(outputs))


def body(
    page_pool,
    move_source,
    move_page,
    move_slot,
    row_count,
    lengths,
    page_table,
    queries,
    value_up,
    out_proj,
    residual,
    norm_gain,
    gate_proj,
    up_proj,
    down_proj,
):
    rank_count = lax.axis_size("dp")
    own_rank = lax.axis_index("dp")
    move_count = move_page.shape[0] // rank_count
    capacity = max(2, (3 * move_count + 2 * rank_count - 1) // (2 * rank_count))
    sources = move_source.reshape(rank_count, move_count)
    page_ids = move_page.reshape(rank_count, move_count)
    slot_ids = move_slot.reshape(rank_count, move_count)
    move_order = jnp.arange(move_count)
    earlier = (sources[:, :, None] == sources[:, None, :]) & (
        move_order[None, None, :] < move_order[None, :, None]
    )
    arrival = jnp.sum(earlier.astype(jnp.int32), axis=2)
    chosen = (sources == own_rank)[:, :, None] & (
        arrival[:, :, None] == jnp.arange(capacity)[None, None, :]
    )
    send_ids = jnp.sum(jnp.where(chosen, page_ids[:, :, None], 0), axis=1)
    page_size = page_pool.shape[1]
    feature_width = page_pool.shape[2]
    outgoing = page_pool[send_ids.reshape(-1)].reshape(
        rank_count, capacity, page_size, feature_width
    )
    incoming = lax.all_to_all(outgoing, "dp", split_axis=0, concat_axis=0, tiled=True)
    own_sources = lax.dynamic_index_in_dim(sources, own_rank, 0, keepdims=False)
    own_arrival = lax.dynamic_index_in_dim(arrival, own_rank, 0, keepdims=False)
    own_slots = lax.dynamic_index_in_dim(slot_ids, own_rank, 0, keepdims=False)
    picked = incoming.reshape(rank_count * capacity, page_size, feature_width)[
        own_sources * capacity + own_arrival
    ]
    local_pool = page_pool.at[own_slots].set(picked)
    rows_local = residual.shape[0]
    valid_rows = jnp.arange(rows_local) < row_count[0]
    latent_out = attend_rows(local_pool, page_table, lengths, queries, valid_rows)
    by_head = lax.all_to_all(latent_out, "dp", split_axis=1, concat_axis=0, tiled=True)
    head_out = jnp.einsum(
        "rhl,hlv->rhv", by_head, value_up, preferred_element_type=jnp.float32
    ).astype(jnp.bfloat16)
    head_out = head_out.reshape(head_out.shape[0], -1)
    rows_slice = head_out
    attention = lax.psum_scatter(
        jnp.dot(rows_slice, out_proj, preferred_element_type=jnp.float32).astype(jnp.bfloat16),
        "dp",
        scatter_dimension=0,
        tiled=True,
    ).astype(jnp.float32)
    middle = residual.astype(jnp.float32) + attention
    normed = rms_scale(middle, norm_gain)
    row_piece = lax.all_gather(normed, "dp", axis=0, tiled=True)
    gate_part = jnp.dot(row_piece, gate_proj, preferred_element_type=jnp.float32)
    up_part = jnp.dot(row_piece, up_proj, preferred_element_type=jnp.float32)
    hidden = (jax.nn.silu(gate_part) * up_part).astype(jnp.bfloat16)
    rows_slice = hidden
    mlp_out = lax.psum_scatter(
        jnp.dot(rows_slice, down_proj, preferred_element_type=jnp.float32).astype(jnp.bfloat16),
        "dp",
        scatter_dimension=0,
        tiled=True,
    ).astype(jnp.float32)
    return (middle + mlp_out).astype(jnp.bfloat16)


def solution(mesh):
    in_specs = (
        P(("rep", "dp"), None, None),
        P("rep", None),
        P("rep"),
        P("rep"),
        P(("rep", "dp")),
        P(("rep", "dp")),
        P(("rep", "dp"), None),
        P(("rep", "dp"), None, None),
        P("dp", None, None),
        P("dp", None),
        P(("rep", "dp"), None),
        P(),
        P(None, "dp"),
        P(None, "dp"),
        P("dp", None),
    )
    out_specs = P(("rep", "dp"), None)
    return jax.shard_map(body, mesh=mesh, in_specs=in_specs, out_specs=out_specs, check_vma=False)
```

profile of v0, /device:TPU:0, one launch (start us, length us, event | category | flops | bytes accessed | tf_op | source)
XLA Modules:
  0.0 549.3 jit_solution(9300526409154306085)
XLA Ops:
  6.5 8.0 %copy.57 = bf16[112,64,576]{2,1,0:T(8,128)(2,1)} copy(bf16[112,64,576]{2,1,0:T(8,128)(2,1)} %param.17) | data formatting | bytes 16515072
  15.4 7.1 %gather_fusion.1 = bf16[64,64,576]{2,1,0:T(8,128)(2,1)} fusion(bf16[112,64,576]{2,1,0:T(8,128)(2,1)} %copy.57, s32[1024]{0:T(1024)S(1)} %pad_clamp_fusion.2), kind=kCustom, calls=%fused_computation.1 | custom fusion | bytes 9437440 | tf_op jit(solution)/shard_map/gather | solution.py:74
  22.5 8.5 %all-to-all-start = ((bf16[32,2,64,576]{3,2,1,0:T(8,128)(2,1)}), bf16[32,2,64,576]{3,2,1,0:T(8,128)(2,1)}, u32[]{:S(2)}, u32[]{:S(2)}) async-start(bf16[32,2,64,576]{3,2,1,0:T(8,128)(2,1)} %bitcast.71), calls=%async_computation | async-start | bytes 10485760 | tf_op jit(solution)/shard_map/all_to_all | solution.py:77
  32.0 64.1 %all-to-all-done = bf16[32,2,64,576]{3,2,1,0:T(8,128)(2,1)} async-done(((bf16[32,2,64,576]{3,2,1,0:T(8,128)(2,1)}), bf16[32,2,64,576]{3,2,1,0:T(8,128)(2,1)}, u32[]{:S(2)}, u32[]{:S(2)}) %all-to-all-start) | async-done | bytes 4718624 | tf_op jit(solution)/shard_map/all_to_all | solution.py:77
  96.1 3.4 gather_fusion.2
  99.6 5.6 %scatter_fusion = bf16[112,64,576]{2,1,0:T(8,128)(2,1)} fusion(bf16[112,64,576]{2,1,0:T(8,128)(2,1)} %copy.57, s32[24]{0:T(128)S(1)} %get-tuple-element.71, bf16[24,64,576]{2,1,0:T(8,128)(2,1)S(1)} %gather_fusion.2), kind=kCustom, calls=%fused_computation.3 | custom fusion | bytes 5308512 | tf_op jit(solution)/shard_map/scatter | solution.py:84
  105.2 157.8 %while.10 = (s32[]{:T(128)}, bf16[16,64,512]{2,1,0:T(8,128)(2,1)}, s32[16]{0:T(128)S(1)}, bf16[16,64,576]{2,1,0:T(8,128)(2,1)}, s32[16,32]{1,0:T(8,128)}, /*index=5*/bf16[112,64,576]{2,1,0:T(8,128)(2,1)}, s32[]{:T(128)}) while((s32[]{:T(128)}, bf16[16,64,512]{2,1,0:T(8,128)(2,1)}, s32[16]{0:T(128)S(1)}, bf16[16,64,576]{2,1,0:T(8,128)(2,1)}, ...), condition=%wide.region_6.7_spmd, body=%wide.region_3.6_spmd.sunk | while | flops 286297056 | bytes 10906977 | solution.py:35
  105.9 4.6 gather_fusion
  111.7 1.9 fusion.48
  113.9 1.2 fusion.50
  115.8 4.6 gather_fusion
  121.6 1.9 fusion.48
  123.8 1.2 fusion.50
  125.6 4.6 gather_fusion
  131.4 1.9 fusion.48
  133.6 1.2 fusion.50
  135.5 4.6 gather_fusion
  141.3 1.9 fusion.48
  145.4 4.6 gather_fusion
  151.2 1.9 fusion.48
  153.3 1.2 fusion.50
  155.2 4.6 gather_fusion
  161.0 1.9 fusion.48
  163.2 1.2 fusion.50
  165.1 4.6 gather_fusion
  170.9 1.9 fusion.48
  173.1 1.2 fusion.50
  174.9 4.6 gather_fusion
  180.8 1.9 fusion.48
  182.9 1.2 fusion.50
  184.8 4.6 gather_fusion
  190.6 1.9 fusion.48
  192.8 1.2 fusion.50
  194.7 4.6 gather_fusion
  200.5 1.9 fusion.48
  202.7 1.2 fusion.50
  204.5 4.6 gather_fusion
  210.4 1.9 fusion.48
  212.5 1.2 fusion.50
  214.4 4.6 gather_fusion
  220.2 1.9 fusion.48
  222.4 1.2 fusion.50
  224.3 4.6 gather_fusion
  230.1 1.9 fusion.48
  232.3 1.2 fusion.50
  234.1 4.6 gather_fusion
  239.9 1.9 fusion.48
  244.0 4.6 gather_fusion
  249.8 1.9 fusion.48
  252.0 1.2 fusion.50
  253.9 4.6 gather_fusion
  259.7 1.9 fusion.48
  261.9 1.2 fusion.50
  263.0 2.0 copy_select_fusion
  265.0 26.2 %all_to_all.23 = bf16[16,64,512]{2,0,1:T(8,128)(2,1)S(1)} all-to-all(bf16[16,64,512]{2,0,1:T(8,128)(2,1)S(1)} %copy_select_fusion), channel_id=1, replica_groups=mesh['dp'=32,'rep'=4] {'dp'}, dimensions={1} | all-to-all | bytes 2097152 | tf_op jit(solution)/shard_map/all_to_all | solution.py:88
  291.8 5.1 convolution_convert_fusion.1
  297.0 86.7 %reduce-scatter.3.cloned.1.call-done = bf16[16,7168]{1,0:T(8,128)(2,1)} async-done(((bf16[512,7168]{1,0:T(8,128)(2,1)}), bf16[16,7168]{1,0:T(8,128)(2,1)}) %reduce-scatter.3.cloned.1.call-update) | async-done | bytes 229392 | tf_op jit(solution)/shard_map/reduce_scatter | solution.py:94
  384.9 1.7 multiply_convert_fusion
  386.9 50.2 %all-gather.2.cloned.1.call-done = bf16[512,7168]{1,0:T(8,128)(2,1)} async-done(((bf16[16,7168]{1,0:T(8,128)(2,1)}), bf16[512,7168]{1,0:T(8,128)(2,1)}) %all-gather.2.cloned.1.call-update) | async-done | bytes 7340048 | tf_op jit(solution)/shard_map/all_gather | solution.py:102
  437.0 6.7 %fusion.27 = f32[512,288]{0,1:T(8,128)S(1)} fusion(bf16[512,7168]{1,0:T(8,128)(2,1)} %all-gather.2.cloned.1.call-done, bf16[7168,288]{0,1:T(8,128)(2,1)} %param.29), kind=kOutput, calls=%fused_computation.55 | convolution fusion | flops 2113929216 | bytes 12058624 | tf_op jit(solution)/shard_map/dot_general | solution.py:103
  444.5 2.6 fusion.20
  447.2 6.1 %convolution_convert_fusion = bf16[512,7168]{1,0:T(8,128)(2,1)} fusion(bf16[512,288]{0,1:T(8,128)(2,1)S(1)} %fusion.20, bf16[288,7168]{1,0:T(8,128)(2,1)S(1)} %copy-done.1), kind=kOutput, calls=%fused_computation.25 | convolution fusion | flops 2117599232 | bytes 11763712 | tf_op jit(solution)/shard_map/dot_general | solution.py:108
  453.3 87.8 %reduce-scatter.5.cloned.1.call-done = bf16[16,7168]{1,0:T(8,128)(2,1)} async-done(((bf16[512,7168]{1,0:T(8,128)(2,1)}), bf16[16,7168]{1,0:T(8,128)(2,1)}) %reduce-scatter.5.cloned.1.call-update) | async-done | bytes 229392 | tf_op jit(solution)/shard_map/reduce_scatter | solution.py:107
  541.1 1.7 add_convert_fusion
  (136 shorter events, 40.3 us)
Async XLA Ops:
  6.5 284.8 %copy-start = (bf16[2,512,128]{2,1,0:T(8,128)(2,1)S(1)}, bf16[2,512,128]{2,1,0:T(8,128)(2,1)}, u32[]{:S(2)}) copy-start(bf16[2,512,128]{2,1,0:T(8,128)(2,1)} %param.25) | copy-start | bytes 786436
  6.5 8.0 %copy-start.8 = (s32[768,1]{0,1:T(1,128)S(1)}, s32[768,1]{0,1:T(1,128)}, u32[]{:S(2)}) copy-start(s32[768,1]{0,1:T(1,128)} %param.18) | copy-start | bytes 9220
  6.5 8.3 %copy-start.6 = (s32[768]{0:T(1024)S(1)}, s32[768]{0:T(1024)}, u32[]{:S(2)}) copy-start(s32[768]{0:T(1024)} %param.19) | copy-start | bytes 9220
  22.5 8.6 %copy-start.7 = (s32[768]{0:T(1024)S(1)}, s32[768]{0:T(1024)}, u32[]{:S(2)}) copy-start(s32[768]{0:T(1024)} %param.20) | copy-start | bytes 9220
  22.5 73.6 %all-to-all-start = ((bf16[32,2,64,576]{3,2,1,0:T(8,128)(2,1)}), bf16[32,2,64,576]{3,2,1,0:T(8,128)(2,1)}, u32[]{:S(2)}, u32[]{:S(2)}) async-start(bf16[32,2,64,576]{3,2,1,0:T(8,128)(2,1)} %bitcast.71), calls=%async_computation | async-start | bytes 10485760 | tf_op jit(solution)/shard_map/all_to_all | solution.py:77
  31.0 352.7 %reduce-scatter.3.cloned.1.call-start = ((), (), s32[]{:S(2)}) async-start(), calls=%async_computation.4 | async-start | bytes 7569408 | tf_op jit(solution)/shard_map/reduce_scatter | solution.py:94
  96.1 9.1 %copy-start.11 = (s32[16]{0:T(128)S(1)}, s32[16]{0:T(128)}, u32[]{:S(2)}) copy-start(s32[16]{0:T(128)} %param.22) | copy-start | bytes 196
  263.0 28.8 %copy-start.2 = (bf16[256,7168]{1,0:T(8,128)(2,1)S(1)}, bf16[256,7168]{1,0:T(8,128)(2,1)}, u32[]{:S(2)}) copy-start(bf16[256,7168]{1,0:T(8,128)(2,1)} %param.26) | copy-start | bytes 11010052
  296.9 86.8 %copy-start.3 = (bf16[16,7168]{1,0:T(8,128)(2,1)S(1)}, bf16[16,7168]{1,0:T(8,128)(2,1)}, u32[]{:S(2)}) copy-start(bf16[16,7168]{1,0:T(8,128)(2,1)} %param.27) | copy-start | bytes 688132
  296.9 87.9 %copy-start.5 = (f32[7168]{0:T(1024)S(1)}, f32[7168]{0:T(1024)}, u32[]{:S(2)}) copy-start(f32[7168]{0:T(1024)} %param.28) | copy-start | bytes 86020
  297.0 140.1 %all-gather.2.cloned.1.call-start = ((), (), s32[]{:S(2)}) async-start(), calls=%async_computation.5 | async-start | bytes 7569408 | tf_op jit(solution)/shard_map/all_gather | solution.py:102
  386.6 154.5 %reduce-scatter.5.cloned.1.call-start = ((), (), s32[]{:S(2)}) async-start(), calls=%async_computation.6 | async-start | bytes 7569408 | tf_op jit(solution)/shard_map/reduce_scatter | solution.py:107
  437.0 6.7 %copy-start.9 = (bf16[512,7168]{1,0:T(8,128)(2,1)S(1)}, bf16[512,7168]{1,0:T(8,128)(2,1)}, u32[]{:S(2)}) copy-start(bf16[512,7168]{1,0:T(8,128)(2,1)} %all-gather.2.cloned.1.call-done) | copy-start | bytes 22020100
  437.0 7.5 %copy-start.10 = (bf16[7168,288]{0,1:T(8,128)(2,1)S(1)}, bf16[7168,288]{0,1:T(8,128)(2,1)}, u32[]{:S(2)}) copy-start(bf16[7168,288]{0,1:T(8,128)(2,1)} %param.30) | copy-start | bytes 12386308
  444.5 2.6 copy-start.1
  453.3 87.8 %copy-start.4 = (bf16[16,7168]{1,0:T(8,128)(2,1)S(1)}, bf16[16,7168]{1,0:T(8,128)(2,1)}, u32[]{:S(2)}) copy-start(bf16[16,7168]{1,0:T(8,128)(2,1)} %reduce-scatter.3.cloned.1.call-done) | copy-start | bytes 688132
Sparse Core Ops, SparseCore 0:
  297.1 86.5 reduce-scatter.2
  386.7 50.2 all-gather.1
  453.4 87.6 reduce-scatter.4
where the time goes:
time: 552 us; the launch traced here: 549 us
  waiting for transfers between devices  289 us (52%)
  local copies, waits for them, and re-layouts  109 us (20%)
  matrix products  70.5 us (13%)
  other arithmetic  31.5 us (6%)
  blocking collectives  26.2 us (5%)
  between operations  14 us (3%)
  starting transfers between devices  8.8 us (2%)
    reduce_scatter x1, waiting for transfers between devices, body(): lax.psum_scatter(jnp.dot(rows_slice, down_proj, preferred_element_type=jn...  87.8 us
    reduce_scatter x1, waiting for transfers between devices, body(): lax.psum_scatter(jnp.dot(rows_slice, out_proj, preferred_element_type=jnp...  86.7 us
    gather x16, local copies, waits for them, and re-layouts, one_row(): tokens = cache_pages[table_row].reshape(-1, cache_pages.shape[2])  74 us
    all_to_all x1, waiting for transfers between devices, body(): lax.all_to_all(outgoing, 'dp', split_axis=0, concat_axis=0, tiled=True)  64.1 us
    all_gather x1, waiting for transfers between devices, body(): row_piece = lax.all_gather(normed, 'dp', axis=0, tiled=True)  50.2 us
    dot_general x16, matrix products, one_row(): jnp.einsum('hk,tk->ht', query_row, tokens, preferred_element_type=jnp.flo...  30.7 us
    all_to_all x1, blocking collectives, body(): lax.all_to_all(latent_out, 'dp', split_axis=1, concat_axis=0, tiled=True)  26.2 us
    dot_general x16, matrix products, one_row(): jnp.einsum('ht,tl->hl', weights, tokens[:, :LATENT], preferred_element_ty...  18.8 us
  transfers between devices with their start and end apart: 4, of which 4 were waited for; matrix products, arithmetic and copies ran while one was open for 0% of the time, Pallas kernels for 0%

commit v1 on v0

v1 whole, which is shorter than its diff:
```python
import functools

import jax
import jax.numpy as jnp
from jax import lax
from jax.experimental import pallas as pl
from jax.experimental.pallas import tpu as pltpu
from jax.sharding import PartitionSpec as P

LATENT = 512
SOFTMAX_SCALE = 192 ** (-0.5)
LOW = -1e30
MESH = pl.DeviceIdType.MESH
F32 = jnp.float32
BF16 = jnp.bfloat16
VMEM_LIMIT = 60 * 2**20
NX = 4
NZ = 4


def vspec():
    return pl.BlockSpec(memory_space=pltpu.VMEM)


def sspec():
    return pl.BlockSpec(memory_space=pltpu.SMEM)


def aspec():
    return pl.BlockSpec(memory_space=pl.ANY)


def pack_kernel(ids_ref, pool_ref, out_ref, sem):
    count = out_ref.shape[0]

    def start(i, carry):
        pltpu.make_async_copy(pool_ref.at[ids_ref[i]], out_ref.at[i], sem).start()
        return carry

    lax.fori_loop(0, count, start, 0)
    pltpu.make_async_copy(out_ref, out_ref, sem).wait()


def pack_pages(ids, pool):
    return pl.pallas_call(
        pack_kernel,
        out_shape=jax.ShapeDtypeStruct((ids.shape[0],) + pool.shape[1:], pool.dtype),
        in_specs=[sspec(), aspec()],
        out_specs=aspec(),
        scratch_shapes=[pltpu.SemaphoreType.DMA],
        name="pack_pages",
    )(ids, pool)


def flash_step(q, pages_ref, entries, carry):
    top, total, acc = carry
    group = len(entries)
    k = jnp.concatenate([pages_ref[e >> 7] for e in entries], axis=0)
    s = lax.dot_general(q, k, (((1,), (1,)), ((), ())), preferred_element_type=F32) * SOFTMAX_SCALE
    col = lax.broadcasted_iota(jnp.int32, (1, 64 * group), 1)
    limit = jnp.zeros((1, 64 * group), jnp.int32)
    for g, e in enumerate(entries):
        limit = jnp.where((col >> 6) == g, e & 127, limit)
    s = jnp.where((col & 63) < limit, s, LOW)
    new_top = jnp.maximum(top, jnp.max(s, axis=1, keepdims=True))
    shrink = jnp.exp(top - new_top)
    p = jnp.exp(s - new_top)
    total = total * shrink + jnp.sum(p, axis=1, keepdims=True)
    acc = acc * shrink + jnp.dot(p.astype(BF16), k[:, :LATENT], preferred_element_type=F32)
    return new_top, total, acc


GROUP_A = 8
GROUP_B = 4
LIST = 40


def local_kernel(table, lens, rc, slots, q_ref, pool_ref, acc_ref, top_ref, total_ref, list_ref, count_ref, slotmap, list_a):
    rows, heads = q_ref.shape[0], q_ref.shape[1]

    def clear(i, carry):
        slotmap[i] = -1
        return carry

    lax.fori_loop(0, pool_ref.shape[0], clear, 0)

    def mark(i, carry):
        slotmap[slots[i]] = i
        return carry

    lax.fori_loop(0, slots.shape[0], mark, 0)

    def row(r, carry):
        length = lens[r]
        pages = jnp.where(r < rc[0], (length + 63) // 64, 0)

        def place(p, c):
            a, b = c
            slot = table[r, p]
            valid = jnp.minimum(length - 64 * p, 64)
            moved = slotmap[slot]
            list_a[a] = slot * 128 + valid
            list_ref[r * LIST + b] = moved * 128 + valid
            is_moved = (moved >= 0).astype(jnp.int32)
            return a + 1 - is_moved, b + is_moved

        a, b = lax.fori_loop(0, pages, place, (0, 0))
        for g in range(GROUP_A):
            list_a[a + g] = 0
        for g in range(GROUP_B):
            list_ref[r * LIST + b + g] = 0
        count_ref[r] = b
        q = q_ref[r]

        def step(i, c):
            return flash_step(q, pool_ref, [list_a[i * GROUP_A + g] for g in range(GROUP_A)], c)

        init = (
            jnp.full((heads, 1), LOW, F32),
            jnp.zeros((heads, 1), F32),
            jnp.zeros((heads, LATENT), F32),
        )
        top, total, acc = lax.fori_loop(0, (a + GROUP_A - 1) // GROUP_A, step, init)
        acc_ref[r] = acc
        top_ref[r] = jnp.broadcast_to(top, (heads, 128))
        total_ref[r] = jnp.broadcast_to(total, (heads, 128))
        return carry

    lax.fori_loop(0, rows, row, 0)


def attend_local(table, lens, rc, slots, queries, pool):
    rows, heads, _ = queries.shape
    return pl.pallas_call(
        local_kernel,
        out_shape=(
            jax.ShapeDtypeStruct((rows, heads, LATENT), F32),
            jax.ShapeDtypeStruct((rows, heads, 128), F32),
            jax.ShapeDtypeStruct((rows, heads, 128), F32),
            jax.ShapeDtypeStruct((rows * LIST,), jnp.int32),
            jax.ShapeDtypeStruct((rows,), jnp.int32),
        ),
        in_specs=[sspec(), sspec(), sspec(), sspec(), vspec(), vspec()],
        out_specs=(vspec(), vspec(), vspec(), sspec(), sspec()),
        scratch_shapes=[pltpu.SMEM((pool.shape[0],), jnp.int32), pltpu.SMEM((LIST + 8,), jnp.int32)],
        compiler_params=pltpu.CompilerParams(vmem_limit_bytes=40 * 2**20),
        cost_estimate=pl.CostEstimate(flops=20_000_000_000, bytes_accessed=14_000_000, transcendentals=2_000_000),
        name="attend_local",
    )(table, lens, rc, slots, queries, pool)


def moved_kernel(list_ref, count_ref, index_ref, q_ref, acc_ref, top_ref, total_ref, in_ref, out_ref, pages, sem):
    rows = q_ref.shape[0]
    count = pages.shape[0]

    def start(i, carry):
        pltpu.make_async_copy(in_ref.at[index_ref[i]], pages.at[i], sem).start()
        return carry

    lax.fori_loop(0, count, start, 0)
    pltpu.make_async_copy(pages, pages, sem).wait()

    def row(r, carry):
        q = q_ref[r]

        def step(i, c):
            return flash_step(q, pages, [list_ref[r * LIST + i * GROUP_B + g] for g in range(GROUP_B)], c)

        init = (top_ref[r][:, :1], total_ref[r][:, :1], acc_ref[r])
        _, total, acc = lax.fori_loop(0, (count_ref[r] + GROUP_B - 1) // GROUP_B, step, init)
        total = jnp.where(total == 0.0, 1.0, total)
        out_ref[r] = (acc / total).astype(BF16)
        return carry

    lax.fori_loop(0, rows, row, 0)


def attend_moved(list_b, count_b, index, queries, acc, top, total, incoming):
    rows, heads, width = queries.shape
    return pl.pallas_call(
        moved_kernel,
        out_shape=jax.ShapeDtypeStruct((rows, heads, LATENT), BF16),
        in_specs=[sspec(), sspec(), sspec(), vspec(), vspec(), vspec(), vspec(), aspec()],
        out_specs=vspec(),
        scratch_shapes=[pltpu.VMEM((index.shape[0], incoming.shape[1], width), BF16), pltpu.SemaphoreType.DMA],
        compiler_params=pltpu.CompilerParams(vmem_limit_bytes=40 * 2**20),
        name="attend_moved",
    )(list_b, count_b, index, queries, acc, top, total, incoming)


SUBS = 2


def tail_kernel(
    lat, vu, wo, res, gain, gate, up, down, out_ref,
    rl, vus, wos, gus, ds, ho, part, nrm, mid, acc, hid,
    b1, b2, c1, c2, e1, e2, f1, f2,
    bar_sems, lat_ss, lat_rs, w_ls, w_ss, w_rs, rs_ss, rs_rs, ag_ss, ag_rs,
):
    me = lax.axis_index("dp")
    core = lax.rem(me, 2)
    chip = me // 2
    x = chip // NZ
    z = lax.rem(chip, NZ)
    cols_all = part.shape[3]
    half = cols_all // 2
    ff = gate.shape[0]

    def device(dx, dz):
        return {"dp": (lax.rem(x + dx + NX, NX) * NZ + lax.rem(z + dz + NZ, NZ)) * 2 + core}

    sibling = {"dp": me + 1 - 2 * core}

    barrier = pltpu.get_barrier_semaphore()
    peers = [(a, b) for a in range(NX) for b in range(NZ) if (a, b) != (0, 0)]
    for a, b in peers:
        pl.semaphore_signal(barrier, inc=1, device_id=device(a, b), device_id_type=MESH)
    pl.semaphore_signal(barrier, inc=1, device_id=sibling, device_id_type=MESH)
    pl.semaphore_wait(barrier, len(peers) + 1)

    sent = []

    def send(src, dst, ss, rs, to):
        copy = pltpu.make_async_remote_copy(
            src_ref=src, dst_ref=dst, send_sem=ss, recv_sem=rs, device_id=to, device_id_type=MESH
        )
        copy.start()
        sent.append(copy)
        return copy

    lat_copies = []
    for k, (a, b) in enumerate(peers):
        to_chip = lax.rem(x + a, NX) * NZ + lax.rem(z + b, NZ)
        lat_copies.append(send(lat.at[to_chip], rl.at[chip], lat_ss.at[k], lat_rs.at[k], device(a, b)))
    own_lat = pltpu.make_async_copy(lat.at[chip], rl.at[chip], bar_sems.at[0])
    own_lat.start()

    row0 = pl.multiple_of(core * ff, 16)
    row1 = pl.multiple_of(640 + core * ff, 16)
    places = [
        (vu, vus.at[core]),
        (wo, wos.at[core]),
        (gate, gus.at[pl.ds(row0, ff), :]),
        (up, gus.at[pl.ds(row1, ff), :]),
        (down, ds.at[pl.ds(row0, ff), :]),
    ]
    w_local, w_remote = [], []
    for k, (src, dst) in enumerate(places):
        copy = pltpu.make_async_copy(src, dst, w_ls.at[k])
        copy.start()
        w_local.append(copy)
        w_remote.append(send(src, dst, w_ss.at[k], w_rs.at[k], sibling))
    gus[pl.ds(2 * ff, 640 - 2 * ff), :] = jnp.zeros((640 - 2 * ff, cols_all), BF16)
    gus[pl.ds(640 + 2 * ff, 640 - 2 * ff), :] = jnp.zeros((640 - 2 * ff, cols_all), BF16)

    def weights_ready(*ks):
        for k in ks:
            w_local[k].wait()
            w_remote[k].wait_recv()

    own_lat.wait()
    for copy in lat_copies:
        copy.wait_recv()
    weights_ready(0)
    for h in range(4):
        l = rl[:, h * 16 : (h + 1) * 16, :].reshape(256, LATENT)
        ho[:, h * 128 : (h + 1) * 128] = jnp.dot(l, vus[h // 2, h % 2], preferred_element_type=F32).astype(BF16)

    width = half // SUBS
    wing = width // 2

    def reduce_scatter(turn, fill, bufs, finish):
        r1, r2, t1, t2 = bufs

        def chunk(h, phase, i, base, size):
            cs = pl.ds(base, size)
            xi, zi = lax.rem(x + i + NX, NX), lax.rem(z + i + NZ, NZ)
            along_x = (h == 0) == (phase == 0)
            if phase == 0:
                return part.at[xi, :, :, cs] if along_x else part.at[:, zi, :, cs]
            return part.at[xi, z, :, cs] if along_x else part.at[x, zi, :, cs]

        def to(h, phase, i):
            return device(i, 0) if (h == 0) == (phase == 0) else device(0, i)

        def sems(h, s, phase, k):
            at = (((turn * 2 + h) * SUBS + s) * 2 + phase) * 6 + k
            return rs_ss.at[at], rs_rs.at[at]

        def bufs_of(h, s, phase):
            first, second = (r1, r2) if phase == 0 else (t1, t2)
            return first.at[h, s], second.at[h, s]

        state = {}

        def start(h, s, phase):
            base = h * half + s * width
            first, second = bufs_of(h, s, phase)
            lo, hi = base, base + wing
            state[h, s, phase] = [
                send(chunk(h, phase, 2, lo, wing), first.at[0], *sems(h, s, phase, 0), to(h, phase, 1)),
                send(chunk(h, phase, 2, hi, wing), first.at[1], *sems(h, s, phase, 1), to(h, phase, -1)),
                send(chunk(h, phase, 1, hi, wing), second.at[0, ..., pl.ds(wing, wing)], *sems(h, s, phase, 2), to(h, phase, 1)),
                send(chunk(h, phase, -1, lo, wing), second.at[1, ..., pl.ds(0, wing)], *sems(h, s, phase, 3), to(h, phase, -1)),
            ]

        def middle(h, s, phase):
            base = h * half + s * width
            first, second = bufs_of(h, s, phase)
            copies = state[h, s, phase]
            for side, (i, at) in enumerate(((1, 0), (-1, wing))):
                copies[side].wait_recv()
                mine = chunk(h, phase, i, base + at, wing)
                mine[...] = (mine[...].astype(F32) + first[side].astype(F32)).astype(BF16)
                copies.append(
                    send(mine, second.at[side, ..., pl.ds(at, wing)], *sems(h, s, phase, 4 + side), to(h, phase, i))
                )

        def total(h, s, phase):
            base = h * half + s * width
            _, second = bufs_of(h, s, phase)
            for copy in state[h, s, phase][2:]:
                copy.wait_recv()
            mine = chunk(h, phase, 0, base, width)
            value = mine[...].astype(F32) + second[0].astype(F32) + second[1].astype(F32)
            if phase == 0:
                mine[...] = value.astype(BF16)
            else:
                finish(base, width, value)

        order = [(h, s) for s in range(SUBS) for h in range(2)]
        for h, s in order:
            fill(h * half + s * width, width)
            start(h, s, 0)
        for h, s in order:
            middle(h, s, 0)
        for h, s in order:
            total(h, s, 0)
            start(h, s, 1)
        for h, s in order:
            middle(h, s, 1)
        for h, s in order:
            total(h, s, 1)

    weights_ready(1)

    def fill_out(base, size):
        cs = pl.ds(base, size)
        v = jnp.dot(ho[:, :256], wos[0, :, cs], preferred_element_type=F32)
        v = v + jnp.dot(ho[:, 256:], wos[1, :, cs], preferred_element_type=F32)
        part[:, :, :, cs] = v.astype(BF16).reshape(NX, NZ, 16, size)

    squares = []

    def finish_out(base, size, value):
        cs = pl.ds(base, size)
        m = res[:, cs].astype(F32) + value
        mid[:, cs] = m
        squares.append(jnp.sum(m * m, axis=1, keepdims=True))

    reduce_scatter(0, fill_out, (b1, b2, c1, c2), finish_out)
    factor = lax.rsqrt(sum(squares) / cols_all + 1e-06)
    nrm[x, z] = (mid[...] * factor * gain[...]).astype(BF16)
    while sent:
        sent.pop().wait_send()

    quarter = half // 2

    def block(h, i, j, lo, size):
        cs = pl.ds(h * half + lo, size)
        dx, dz = (j, i) if h == 0 else (i, j)
        return nrm.at[lax.rem(x + dx + NX, NX), lax.rem(z + dz + NZ, NZ), :, cs]

    def ag_sems(h, k):
        return ag_ss.at[h * 20 + k], ag_rs.at[h * 20 + k]

    def along(h, first, i):
        return device(0, i) if (h == 0) == first else device(i, 0)

    def pass_on(ref, h, k, first, i):
        return send(ref, ref, *ag_sems(h, k), along(h, first, i))

    one, two = {}, {}
    for h in range(2):
        ref = block(h, 0, 0, 0, half)
        one[h] = [pass_on(ref, h, 0, True, 1), pass_on(ref, h, 1, True, -1)]

    def spread(h, n, i):
        ref = block(h, i, 0, 0, half)
        two[h, n] = [pass_on(ref, h, 4 + 4 * n, False, 1), pass_on(ref, h, 5 + 4 * n, False, -1)]

    def forward(h, n, i):
        two[h, n][0].wait_recv()
        two[h, n].append(pass_on(block(h, i, -1, 0, quarter), h, 6 + 4 * n, False, 1))
        two[h, n][1].wait_recv()
        two[h, n].append(pass_on(block(h, i, 1, quarter, quarter), h, 7 + 4 * n, False, -1))

    for h in range(2):
        spread(h, 0, 0)
    for h in range(2):
        one[h][0].wait_recv()
        one[h].append(pass_on(block(h, -1, 0, 0, quarter), h, 2, True, 1))
        one[h][1].wait_recv()
        one[h].append(pass_on(block(h, 1, 0, quarter, quarter), h, 3, True, -1))
        spread(h, 1, -1)
        spread(h, 2, 1)
    for h in range(2):
        forward(h, 0, 0)
    for h in range(2):
        one[h][2].wait_recv()
        one[h][3].wait_recv()
        spread(h, 3, 2)
    for n, i in ((1, -1), (2, 1), (3, 2)):
        for h in range(2):
            forward(h, n, i)
    for h in range(2):
        for n in range(4):
            two[h, n][2].wait_recv()
            two[h, n][3].wait_recv()

    weights_ready(2, 3)
    depth = cols_all // 4

    def up_step(k, carry):
        cs = pl.ds(pl.multiple_of(k * depth, 128), depth)
        v = lax.dot_general(
            nrm[:, :, :, cs].reshape(256, depth), gus[:, cs], (((1,), (1,)), ((), ())), preferred_element_type=F32
        )

        @pl.when(k == 0)
        def _():
            acc[...] = v

        @pl.when(k > 0)
        def _():
            acc[...] += v

        return carry

    lax.fori_loop(0, 4, up_step, 0)
    g = acc[:, :640]
    hid[...] = (g / (1.0 + jnp.exp(-g)) * acc[:, 640:]).astype(BF16)
    weights_ready(4)

    def fill_down(base, size):
        cs = pl.ds(base, size)
        v = jnp.dot(hid[:, : 2 * ff], ds[:, cs], preferred_element_type=F32)
        part[:, :, :, cs] = v.astype(BF16).reshape(NX, NZ, 16, size)

    def finish_down(base, size, value):
        cs = pl.ds(base, size)
        out_ref[:, cs] = (mid[:, cs] + value).astype(BF16)

    reduce_scatter(1, fill_down, (e1, e2, f1, f2), finish_down)
    while sent:
        sent.pop().wait_send()


def tail(lat, value_up, out_proj, residual, norm_gain, gate_t, up_t, down):
    cols = residual.shape[1]
    ff = gate_t.shape[0]
    width = cols // 2 // SUBS
    rs_bufs = [
        pltpu.VMEM((2, SUBS, 2, 4, 16, width // 2), BF16),
        pltpu.VMEM((2, SUBS, 2, 4, 16, width), BF16),
        pltpu.VMEM((2, SUBS, 2, 16, width // 2), BF16),
        pltpu.VMEM((2, SUBS, 2, 16, width), BF16),
    ]
    n_rs = 2 * 2 * SUBS * 2 * 6
    dma = pltpu.SemaphoreType.DMA
    return pl.pallas_call(
        tail_kernel,
        out_shape=jax.ShapeDtypeStruct(residual.shape, BF16),
        in_specs=[aspec(), aspec(), aspec(), vspec(), vspec(), aspec(), aspec(), aspec()],
        out_specs=vspec(),
        scratch_shapes=[
            pltpu.VMEM((16, 64, LATENT), BF16),
            pltpu.VMEM((2, 2, LATENT, 128), BF16),
            pltpu.VMEM((2, 256, cols), BF16),
            pltpu.VMEM((1280, cols), BF16),
            pltpu.VMEM((2 * ff, cols), BF16),
            pltpu.VMEM((256, 512), BF16),
            pltpu.VMEM((NX, NZ, 16, cols), BF16),
            pltpu.VMEM((NX, NZ, 16, cols), BF16),
            pltpu.VMEM((16, cols), F32),
            pltpu.VMEM((256, 1280), F32),
            pltpu.VMEM((256, 640), BF16),
            *rs_bufs,
            *rs_bufs,
            dma((1,)),
            dma((15,)),
            dma((15,)),
            dma((5,)),
            dma((5,)),
            dma((5,)),
            dma((n_rs,)),
            dma((n_rs,)),
            dma((40,)),
            dma((40,)),
        ],
        compiler_params=pltpu.CompilerParams(collective_id=0, has_side_effects=True, vmem_limit_bytes=VMEM_LIMIT),
        cost_estimate=pl.CostEstimate(flops=12_000_000_000, bytes_accessed=40_000_000, transcendentals=200_000),
        name="tail",
    )(lat, value_up, out_proj, residual, norm_gain.reshape(1, cols), gate_t, up_t, down)


def body(
    page_pool,
    move_source,
    move_page,
    move_slot,
    row_count,
    lengths,
    page_table,
    queries,
    value_up,
    out_proj,
    residual,
    norm_gain,
    gate_proj,
    up_proj,
    down_proj,
):
    rank_count = lax.axis_size("dp")
    own_rank = lax.axis_index("dp")
    move_count = move_page.shape[0] // rank_count
    capacity = 2
    sources = move_source.reshape(rank_count, move_count)
    page_ids = move_page.reshape(rank_count, move_count)
    slot_ids = move_slot.reshape(rank_count, move_count)
    move_order = jnp.arange(move_count)
    earlier = (sources[:, :, None] == sources[:, None, :]) & (
        move_order[None, None, :] < move_order[None, :, None]
    )
    arrival = jnp.sum(earlier.astype(jnp.int32), axis=2)
    chosen = (sources == own_rank)[:, :, None] & (
        arrival[:, :, None] == jnp.arange(capacity)[None, None, :]
    )
    send_ids = jnp.sum(jnp.where(chosen, page_ids[:, :, None], 0), axis=1).reshape(-1)
    page_shape = page_pool.shape[1:]
    outgoing = pack_pages(send_ids, page_pool).reshape((rank_count, capacity) + page_shape)
    incoming = lax.all_to_all(outgoing, "dp", split_axis=0, concat_axis=0, tiled=True)
    own_sources = lax.dynamic_index_in_dim(sources, own_rank, 0, keepdims=False)
    own_arrival = lax.dynamic_index_in_dim(arrival, own_rank, 0, keepdims=False)
    own_slots = lax.dynamic_index_in_dim(slot_ids, own_rank, 0, keepdims=False)
    acc, top, total, list_b, count_b = attend_local(
        page_table, lengths, row_count, own_slots, queries, page_pool
    )
    latent = attend_moved(
        list_b, count_b, own_sources * capacity + own_arrival, queries, acc, top, total,
        incoming.reshape((rank_count * capacity,) + page_shape),
    )
    rows, heads, _ = latent.shape
    lat = latent.reshape(rows, NX * NZ, heads // (NX * NZ), LATENT).transpose(1, 2, 0, 3)
    lat = lat.reshape(NX * NZ, -1, LATENT)
    return tail(lat, value_up, out_proj, residual, norm_gain, gate_proj.T, up_proj.T, down_proj)


def solution(mesh):
    in_specs = (
        P(("rep", "dp"), None, None),
        P("rep", None),
        P("rep"),
        P("rep"),
        P(("rep", "dp")),
        P(("rep", "dp")),
        P(("rep", "dp"), None),
        P(("rep", "dp"), None, None),
        P("dp", None, None),
        P("dp", None),
        P(("rep", "dp"), None),
        P(),
        P(None, "dp"),
        P(None, "dp"),
        P("dp", None),
    )
    out_specs = P(("rep", "dp"), None)
    return jax.shard_map(body, mesh=mesh, in_specs=in_specs, out_specs=out_specs, check_vma=False)
```

time: 552 us -> 363 us (0.66)
  Pallas kernels: 0 us -> 285 us
  waiting for transfers between devices: 289 us -> 54.6 us
  local copies, waits for them, and re-layouts: 109 us -> 12.4 us
  matrix products: 70.5 us -> 0 us
  other arithmetic: 31.5 us -> 1.08 us
  blocking collectives: 26.2 us -> 0 us
  between operations: 14 us -> 0.82 us
    pallas_call x0 -> x4, Pallas kernels: none -> 285 us  [the longest x1 161 us: pack_pages(): pl.pallas_call(pack_kernel, out_shape=jax.ShapeDtypeStruct((ids.shape[0],...]
    reduce_scatter x2 -> x0, waiting for transfers between devices: 174 us -> none  [the longest x1 87.8 us: body(): lax.psum_scatter(jnp.dot(rows_slice, down_proj, preferred_element_type=jn...]
    gather x18 -> x0, local copies, waits for them, and re-layouts: 84.5 us -> none  [the longest x16 74 us: one_row(): tokens = cache_pages[table_row].reshape(-1, cache_pages.shape[2])]
    dot_general x37 -> x0, matrix products: 70.5 us -> none  [the longest x16 30.7 us: one_row(): jnp.einsum('hk,tk->ht', query_row, tokens, preferred_element_type=jnp.flo...]
    all_gather x1 -> x0, waiting for transfers between devices: 50.2 us -> none  [body(): row_piece = lax.all_gather(normed, 'dp', axis=0, tiled=True)]
    all_to_all x1 -> x0, blocking collectives: 26.2 us -> none  [body(): lax.all_to_all(latent_out, 'dp', split_axis=1, concat_axis=0, tiled=True)]
    select_n x19 -> x0, other arithmetic: 13.1 us -> none  [the longest x16 11.1 us: one_row(): tokens = cache_pages[table_row].reshape(-1, cache_pages.shape[2])]
    all_to_all x1, waiting for transfers between devices: 64.1 us -> 54.6 us  [body(): lax.all_to_all(outgoing, 'dp', split_axis=0, concat_axis=0, tiled=True)]
  transfers between devices with their start and end apart: 4 -> 1, of which waited for: 4 -> 1; matrix products, arithmetic and copies ran while one was open for 0% -> 0% of each run, Pallas kernels for 0% -> 1%
where the time goes in v1:
time: 363 us; the launch traced here: 362 us
  Pallas kernels  285 us (79%)
  waiting for transfers between devices  54.6 us (15%)
  local copies, waits for them, and re-layouts  12.4 us (3%)
  starting transfers between devices  8.51 us (2%)
    pallas_call x1, Pallas kernels, pack_pages(): pl.pallas_call(pack_kernel, out_shape=jax.ShapeDtypeStruct((ids.shape[0],...  161 us
    pallas_call x1, Pallas kernels, tail(): pl.pallas_call(tail_kernel, out_shape=jax.ShapeDtypeStruct(residual.shape...  116 us
    all_to_all x1, waiting for transfers between devices, body(): lax.all_to_all(outgoing, 'dp', split_axis=0, concat_axis=0, tiled=True)  54.6 us
    unnamed x19, local copies, waits for them, and re-layouts  8.98 us
    all_to_all x1, starting transfers between devices, body(): lax.all_to_all(outgoing, 'dp', split_axis=0, concat_axis=0, tiled=True)  8.51 us
  transfers between devices with their start and end apart: 1, of which 1 were waited for; matrix products, arithmetic and copies ran while one was open for 0% of the time, Pallas kernels for 1%

profile of v1, /device:TPU:0, one launch (start us, length us, event | category | flops | bytes accessed | tf_op | source)
XLA Modules:
  0.0 362.1 jit_solution(623933790982472570)
XLA Ops:
  0.0 0.7 reduce
  0.7 0.1 reshape.52
  0.8 0.1 copy.25
  0.9 0.1 copy.28
  1.0 0.8 broadcast_in_dim.19
  1.7 0.1 copy.29
  1.8 0.2 convert_reduce_fusion
  2.0 0.1 copy.30
  2.1 0.6 reshape.53.ids_ref
  2.7 160.6 %pack_pages.1 = bf16[64,64,576]{2,1,0:T(8,128)(2,1)} custom-call(s32[64]{0:T(128)} %reshape.53.ids_ref, bf16[112,64,576]{2,1,0:T(8,128)(2,1)} %pool_ref.3), custom_call_target="tpu_custom_call" | custom-call | tf_op jit(solution)/shard_map/pack_pages/pallas_call | solution.py:45
  163.3 0.0 copy-start.8
  163.3 0.0 copy-start.1
  163.3 0.0 copy-start.6
  163.4 0.0 copy-start.7
  163.4 8.5 %all-to-all-start = ((bf16[32,2,64,576]{3,2,1,0:T(8,128)(2,1)}), bf16[32,2,64,576]{3,2,1,0:T(8,128)(2,1)}, u32[]{:S(2)}, u32[]{:S(2)}) async-start(bf16[32,2,64,576]{3,2,1,0:T(8,128)(2,1)} %bitcast.12), calls=%async_computation | async-start | bytes 10485760 | tf_op jit(solution)/shard_map/all_to_all | solution.py:542
  172.5 0.0 copy-done.8
  172.5 0.1 reshape.51
  172.6 0.2 add_reduce_fusion.index_ref
  172.8 0.0 copy-done.1
  172.8 0.0 copy-done.6
  172.9 0.0 copy-done.7
  172.9 0.0 copy-start
  172.9 3.6 copy-done
  176.5 4.3 %attend_local.1 = (f32[16,64,512]{2,1,0:T(8,128)S(1)}, f32[16,64,128]{2,1,0:T(8,128)S(1)}, f32[16,64,128]{2,1,0:T(8,128)S(1)}, s32[640]{0:T(1024)S(1)}, s32[16]{0:T(128)S(1)}) custom-call(s32[16,32]{1,0:T(8,128)S(1)} %copy-done.6, s32[16]{0:T(128)S(1)} %copy-done.7, s32[1]{0:T(128)S(6)} %copy.34.rc, s32[24]{0:T(128)S(1)} %fusion.1.slots, ...), custom_call_target="tpu_custom_call" | custom-call | flops 20000000000 | bytes 14000000 | tf_op jit(solution)/shard_map/attend_local/pallas_call | solution.py:134
  180.8 0.0 copy-start.2
  180.8 0.8 copy-done.2
  181.6 0.0 copy-start.4
  181.7 0.8 copy-done.4
  182.5 54.6 %all-to-all-done = bf16[32,2,64,576]{3,2,1,0:T(8,128)(2,1)} async-done(((bf16[32,2,64,576]{3,2,1,0:T(8,128)(2,1)}), bf16[32,2,64,576]{3,2,1,0:T(8,128)(2,1)}, u32[]{:S(2)}, u32[]{:S(2)}) %all-to-all-start) | async-done | bytes 4718624 | tf_op jit(solution)/shard_map/all_to_all | solution.py:542
  237.0 0.0 copy-start.3
  237.0 1.0 copy-done.3
  238.1 0.0 copy-start.5
  238.1 1.0 copy-done.5
  239.1 3.8 %attend_moved.1 = bf16[16,64,512]{2,1,0:T(8,128)(2,1)S(1)} custom-call(s32[640]{0:T(1024)S(1)} %get-tuple-element.10.list_ref, s32[16]{0:T(128)S(1)} %get-tuple-element.11.count_ref, s32[24]{0:T(128)S(1)} %add_reduce_fusion.index_ref, bf16[16,64,576]{2,1,0:T(8,128)(2,1)S(1)} %copy-done.1, f32[16,64,512]{2,1,0:T(8,128)S(1)} %get-tuple-element.12.acc_ref, ...), custom_call_target="tpu_custom_call" | custom-call | tf_op jit(solution)/shard_map/attend_moved/pallas_call | solution.py:180
  242.9 1.6 copy.32
  244.5 115.9 %tail.1 = bf16[16,7168]{1,0:T(8,128)(2,1)} custom-call(bf16[16,64,512]{2,1,0:T(8,128)(2,1)} %bitcast.13, bf16[2,512,128]{2,1,0:T(8,128)(2,1)} %vu.1, bf16[256,7168]{1,0:T(8,128)(2,1)} %wo.1, bf16[16,7168]{1,0:T(8,128)(2,1)} %res.1, f32[1,7168]{1,0:T(1,128)} %bitcast.16, bf16[288,7168]{1,0:T(8,128)(2,1)} %bitcast.14, bf16[288,7168]{1,0:T(8,128)(2,1)} %bitcast.15, ...), custom_call_target="tpu_custom_call" | custom-call | flops 12000000000 | bytes 40000000 | tf_op jit(solution)/shard_map/tail/pallas_call | solution.py:471
  360.4 1.6 copy.35
  (4 shorter events, 0.0 us)
Async XLA Ops:
  163.3 9.2 %copy-start.8 = (s32[768]{0:T(1024)S(1)}, s32[768]{0:T(1024)}, u32[]{:S(2)}) copy-start(s32[768]{0:T(1024)} %param.18) | copy-start | bytes 9220
  163.3 9.5 %copy-start.1 = (bf16[16,64,576]{2,1,0:T(8,128)(2,1)S(1)}, bf16[16,64,576]{2,1,0:T(8,128)(2,1)}, u32[]{:S(2)}) copy-start(bf16[16,64,576]{2,1,0:T(8,128)(2,1)} %q_ref.3) | copy-start | bytes 3538948
  163.3 9.5 %copy-start.6 = (s32[16,32]{1,0:T(8,128)S(1)}, s32[16,32]{1,0:T(8,128)}, u32[]{:S(2)}) copy-start(s32[16,32]{1,0:T(8,128)} %table.1) | copy-start | bytes 6148
  163.4 9.5 %copy-start.7 = (s32[16]{0:T(128)S(1)}, s32[16]{0:T(128)}, u32[]{:S(2)}) copy-start(s32[16]{0:T(128)} %lens.1) | copy-start | bytes 196
  163.4 73.7 %all-to-all-start = ((bf16[32,2,64,576]{3,2,1,0:T(8,128)(2,1)}), bf16[32,2,64,576]{3,2,1,0:T(8,128)(2,1)}, u32[]{:S(2)}, u32[]{:S(2)}) async-start(bf16[32,2,64,576]{3,2,1,0:T(8,128)(2,1)} %bitcast.12), calls=%async_computation | async-start | bytes 10485760 | tf_op jit(solution)/shard_map/all_to_all | solution.py:542
  172.9 3.6 copy-start
  180.8 0.8 copy-start.2
  181.6 0.8 copy-start.4
  237.0 1.0 copy-start.3
  238.1 1.0 copy-start.5

commit v2 on v1

--- a/solution.py
+++ b/solution.py
@@ -30,24 +30,25 @@
     return pl.BlockSpec(memory_space=pl.ANY)
 
 
-def pack_kernel(ids_ref, pool_ref, out_ref, sem):
-    count = out_ref.shape[0]
-
-    def start(i, carry):
-        pltpu.make_async_copy(pool_ref.at[ids_ref[i]], out_ref.at[i], sem).start()
-        return carry
-
-    lax.fori_loop(0, count, start, 0)
-    pltpu.make_async_copy(out_ref, out_ref, sem).wait()
+def pack_kernel(ids_ref, pool_ref, out_ref):
+    def pair(i, carry):
+        one, two = pool_ref[ids_ref[2 * i]], pool_ref[ids_ref[2 * i + 1]]
+        out_ref[i, :, :LATENT] = one[:, :LATENT]
+        out_ref[i, :, LATENT : 2 * LATENT] = two[:, :LATENT]
+        out_ref[i, :, 2 * LATENT :] = jnp.concatenate([one[:, LATENT:], two[:, LATENT:]], axis=1)
+        return carry
+
+    lax.fori_loop(0, out_ref.shape[0], pair, 0)
 
 
 def pack_pages(ids, pool):
+    _, page, width = pool.shape
     return pl.pallas_call(
         pack_kernel,
-        out_shape=jax.ShapeDtypeStruct((ids.shape[0],) + pool.shape[1:], pool.dtype),
-        in_specs=[sspec(), aspec()],
-        out_specs=aspec(),
-        scratch_shapes=[pltpu.SemaphoreType.DMA],
+        out_shape=jax.ShapeDtypeStruct((ids.shape[0] // 2, page, 2 * width), pool.dtype),
+        in_specs=[sspec(), vspec()],
+        out_specs=vspec(),
+        compiler_params=pltpu.CompilerParams(vmem_limit_bytes=40 * 2**20),
         name="pack_pages",
     )(ids, pool)
 
@@ -149,16 +150,25 @@
     )(table, lens, rc, slots, queries, pool)
 
 
-def moved_kernel(list_ref, count_ref, index_ref, q_ref, acc_ref, top_ref, total_ref, in_ref, out_ref, pages, sem):
+def moved_kernel(list_ref, count_ref, index_ref, q_ref, acc_ref, top_ref, total_ref, in_ref, out_ref, pairs, pages, sem):
     rows = q_ref.shape[0]
     count = pages.shape[0]
 
     def start(i, carry):
-        pltpu.make_async_copy(in_ref.at[index_ref[i]], pages.at[i], sem).start()
+        pltpu.make_async_copy(in_ref.at[index_ref[i] >> 1], pairs.at[i], sem).start()
         return carry
 
     lax.fori_loop(0, count, start, 0)
-    pltpu.make_async_copy(pages, pages, sem).wait()
+    pltpu.make_async_copy(pairs, pairs, sem).wait()
+
+    def unpack(i, carry):
+        first = (index_ref[i] & 1) == 0
+        pages[i, :, :LATENT] = jnp.where(first, pairs[i, :, :LATENT], pairs[i, :, LATENT : 2 * LATENT])
+        turned = pairs[i, :, 2 * LATENT :]
+        pages[i, :, LATENT:] = jnp.where(first, turned[:, : pages.shape[2] - LATENT], turned[:, pages.shape[2] - LATENT :])
+        return carry
+
+    lax.fori_loop(0, count, unpack, 0)
 
     def row(r, carry):
         q = q_ref[r]
@@ -182,7 +192,11 @@
         out_shape=jax.ShapeDtypeStruct((rows, heads, LATENT), BF16),
         in_specs=[sspec(), sspec(), sspec(), vspec(), vspec(), vspec(), vspec(), aspec()],
         out_specs=vspec(),
-        scratch_shapes=[pltpu.VMEM((index.shape[0], incoming.shape[1], width), BF16), pltpu.SemaphoreType.DMA],
+        scratch_shapes=[
+            pltpu.VMEM((index.shape[0],) + incoming.shape[1:], BF16),
+            pltpu.VMEM((index.shape[0], incoming.shape[1], width), BF16),
+            pltpu.SemaphoreType.DMA,
+        ],
         compiler_params=pltpu.CompilerParams(vmem_limit_bytes=40 * 2**20),
         name="attend_moved",
     )(list_b, count_b, index, queries, acc, top, total, incoming)
@@ -537,8 +551,7 @@
         arrival[:, :, None] == jnp.arange(capacity)[None, None, :]
     )
     send_ids = jnp.sum(jnp.where(chosen, page_ids[:, :, None], 0), axis=1).reshape(-1)
-    page_shape = page_pool.shape[1:]
-    outgoing = pack_pages(send_ids, page_pool).reshape((rank_count, capacity) + page_shape)
+    outgoing = pack_pages(send_ids, page_pool)
     incoming = lax.all_to_all(outgoing, "dp", split_axis=0, concat_axis=0, tiled=True)
     own_sources = lax.dynamic_index_in_dim(sources, own_rank, 0, keepdims=False)
     own_arrival = lax.dynamic_index_in_dim(arrival, own_rank, 0, keepdims=False)
@@ -547,8 +560,7 @@
         page_table, lengths, row_count, own_slots, queries, page_pool
     )
     latent = attend_moved(
-        list_b, count_b, own_sources * capacity + own_arrival, queries, acc, top, total,
-        incoming.reshape((rank_count * capacity,) + page_shape),
+        list_b, count_b, own_sources * capacity + own_arrival, queries, acc, top, total, incoming
     )
     rows, heads, _ = latent.shape
     lat = latent.reshape(rows, NX * NZ, heads // (NX * NZ), LATENT).transpose(1, 2, 0, 3)

time: 363 us -> 206 us (0.57)
  Pallas kernels: 285 us -> 153 us
  waiting for transfers between devices: 54.6 us -> 24.2 us
  local copies, waits for them, and re-layouts: 12.4 us -> 17.6 us
    pallas_call x1, Pallas kernels: 161 us -> 3 us  [pack_pages(): pl.pallas_call(pack_kernel, out_shape=jax.ShapeDtypeStruct((ids.shape[0]...]
    all_to_all x1, waiting for transfers between devices: 54.6 us -> 24.2 us  [body(): lax.all_to_all(outgoing, 'dp', split_axis=0, concat_axis=0, tiled=True)]
    pallas_call x1, Pallas kernels: 4.34 us -> 28.6 us  [attend_local(): pl.pallas_call(local_kernel, out_shape=(jax.ShapeDtypeStruct((rows, heads...]
    pallas_call x1, Pallas kernels: 3.82 us -> 18.6 us  [attend_moved(): pl.pallas_call(moved_kernel, out_shape=jax.ShapeDtypeStruct((rows, heads,...]
    pallas_call x1, Pallas kernels: 116 us -> 103 us  [tail(): pl.pallas_call(tail_kernel, out_shape=jax.ShapeDtypeStruct(residual.shape...]
    unnamed x19 -> x23, local copies, waits for them, and re-layouts: 8.98 us -> 14.7 us
  transfers between devices with their start and end apart: 1 -> 1, of which waited for: 1 -> 1; matrix products, arithmetic and copies ran while one was open for 0% -> 0% of each run, Pallas kernels for 1% -> 14%
where the time goes in v2:
time: 206 us; the launch traced here: 205 us
  Pallas kernels  153 us (74%)
  waiting for transfers between devices  24.2 us (12%)
  local copies, waits for them, and re-layouts  17.6 us (9%)
  starting transfers between devices  8.51 us (4%)
    pallas_call x1, Pallas kernels, tail(): pl.pallas_call(tail_kernel, out_shape=jax.ShapeDtypeStruct(residual.shape...  103 us
    pallas_call x1, Pallas kernels, attend_local(): pl.pallas_call(local_kernel, out_shape=(jax.ShapeDtypeStruct((rows, heads...  28.6 us
    all_to_all x1, waiting for transfers between devices, body(): lax.all_to_all(outgoing, 'dp', split_axis=0, concat_axis=0, tiled=True)  24.2 us
    pallas_call x1, Pallas kernels, attend_moved(): pl.pallas_call(moved_kernel, out_shape=jax.ShapeDtypeStruct((rows, heads,...  18.6 us
    unnamed x23, local copies, waits for them, and re-layouts  14.7 us
    all_to_all x1, starting transfers between devices, body(): lax.all_to_all(outgoing, 'dp', split_axis=0, concat_axis=0, tiled=True)  8.51 us
  transfers between devices with their start and end apart: 1, of which 1 were waited for; matrix products, arithmetic and copies ran while one was open for 0% of the time, Pallas kernels for 14%

profile of v2, /device:TPU:0, one launch (start us, length us, event | category | flops | bytes accessed | tf_op | source)
XLA Modules:
  0.0 205.2 jit_solution(17734842314522138118)
XLA Ops:
  0.0 0.7 reduce
  0.7 0.1 reshape.46
  0.8 0.1 copy.25
  0.9 0.1 copy.28
  1.0 0.8 broadcast_in_dim.19
  1.7 0.1 copy.29
  1.8 0.2 convert_reduce_fusion
  2.0 0.1 copy.30
  2.1 0.1 reshape.47.ids_ref
  2.2 0.0 copy-start.1
  2.2 3.6 %copy-done.1 = bf16[112,64,576]{2,1,0:T(8,128)(2,1)S(1)} copy-done((bf16[112,64,576]{2,1,0:T(8,128)(2,1)S(1)}, bf16[112,64,576]{2,1,0:T(8,128)(2,1)}, u32[]{:S(2)}) %copy-start.1) | copy-done | bytes 8257560
  5.8 3.0 %pack_pages.1 = bf16[32,64,1152]{2,1,0:T(8,128)(2,1)S(1)} custom-call(s32[64]{0:T(128)S(1)} %reshape.47.ids_ref, bf16[112,64,576]{2,1,0:T(8,128)(2,1)S(1)} %copy-done.1), custom_call_target="tpu_custom_call" | custom-call | tf_op jit(solution)/shard_map/pack_pages/pallas_call | solution.py:46
  8.8 0.0 copy-start
  8.8 2.2 %copy-done = bf16[32,64,1152]{2,1,0:T(8,128)(2,1)} copy-done((bf16[32,64,1152]{2,1,0:T(8,128)(2,1)}, bf16[32,64,1152]{2,1,0:T(8,128)(2,1)S(1)}, u32[]{:S(2)}) %copy-start) | copy-done | bytes 4718616
  11.0 0.0 copy-start.10
  11.0 0.0 copy-start.3
  11.0 0.0 copy-start.8
  11.0 0.0 copy-start.9
  11.0 8.5 %all-to-all-start = ((bf16[32,64,1152]{2,1,0:T(8,128)(2,1)}), bf16[32,64,1152]{2,1,0:T(8,128)(2,1)}, u32[]{:S(2)}, u32[]{:S(2)}) async-start(bf16[32,64,1152]{2,1,0:T(8,128)(2,1)} %copy-done), calls=%async_computation | async-start | bytes 9437184 | tf_op jit(solution)/shard_map/all_to_all | solution.py:555
  20.2 0.0 copy-done.10
  20.2 0.1 reshape.45
  20.3 0.2 add_reduce_fusion.index_ref
  20.5 0.0 copy-done.3
  20.5 0.0 copy-done.8
  20.5 0.0 copy-done.9
  20.5 0.0 copy-start.2
  20.5 3.6 %copy-done.2 = bf16[112,64,576]{2,1,0:T(8,128)(2,1)S(1)} copy-done((bf16[112,64,576]{2,1,0:T(8,128)(2,1)S(1)}, bf16[112,64,576]{2,1,0:T(8,128)(2,1)}, u32[]{:S(2)}) %copy-start.2) | copy-done | bytes 8257560
  24.1 28.6 %attend_local.1 = (f32[16,64,512]{2,1,0:T(8,128)S(1)}, f32[16,64,128]{2,1,0:T(8,128)S(1)}, f32[16,64,128]{2,1,0:T(8,128)S(1)}, s32[640]{0:T(1024)S(1)}, s32[16]{0:T(128)S(1)}) custom-call(s32[16,32]{1,0:T(8,128)S(1)} %copy-done.8, s32[16]{0:T(128)S(1)} %copy-done.9, s32[1]{0:T(128)S(6)} %copy.34.rc, s32[24]{0:T(128)S(1)} %fusion.1.slots, ...), custom_call_target="tpu_custom_call" | custom-call | flops 20000000000 | bytes 14000000 | tf_op jit(solution)/shard_map/attend_local/pallas_call | solution.py:135
  52.7 0.0 copy-start.4
  52.7 0.8 copy-done.4
  53.5 0.0 copy-start.6
  53.5 0.8 copy-done.6
  54.2 24.2 %all-to-all-done.in_ref = bf16[32,64,1152]{2,1,0:T(8,128)(2,1)} async-done(((bf16[32,64,1152]{2,1,0:T(8,128)(2,1)}), bf16[32,64,1152]{2,1,0:T(8,128)(2,1)}, u32[]{:S(2)}, u32[]{:S(2)}) %all-to-all-start) | async-done | bytes 4718624 | tf_op jit(solution)/shard_map/all_to_all | solution.py:555
  78.5 0.0 copy-start.5
  78.5 1.0 copy-done.5
  79.5 0.0 copy-start.7
  79.5 1.0 copy-done.7
  80.6 18.6 %attend_moved.1 = bf16[16,64,512]{2,1,0:T(8,128)(2,1)S(1)} custom-call(s32[640]{0:T(1024)S(1)} %get-tuple-element.10.list_ref, s32[16]{0:T(128)S(1)} %get-tuple-element.11.count_ref, s32[24]{0:T(128)S(1)} %add_reduce_fusion.index_ref, bf16[16,64,576]{2,1,0:T(8,128)(2,1)S(1)} %copy-done.3, f32[16,64,512]{2,1,0:T(8,128)S(1)} %get-tuple-element.12.acc_ref, ...), custom_call_target="tpu_custom_call" | custom-call | tf_op jit(solution)/shard_map/attend_moved/pallas_call | solution.py:190
  99.2 1.6 copy.32
  100.7 102.8 %tail.1 = bf16[16,7168]{1,0:T(8,128)(2,1)} custom-call(bf16[16,64,512]{2,1,0:T(8,128)(2,1)} %bitcast.10, bf16[2,512,128]{2,1,0:T(8,128)(2,1)} %vu.1, bf16[256,7168]{1,0:T(8,128)(2,1)} %wo.1, bf16[16,7168]{1,0:T(8,128)(2,1)} %res.1, f32[1,7168]{1,0:T(1,128)} %bitcast.13, bf16[288,7168]{1,0:T(8,128)(2,1)} %bitcast.11, bf16[288,7168]{1,0:T(8,128)(2,1)} %bitcast.12, ...), custom_call_target="tpu_custom_call" | custom-call | flops 12000000000 | bytes 40000000 | tf_op jit(solution)/shard_map/tail/pallas_call | solution.py:485
  203.5 1.6 copy.35
  (4 shorter events, 0.0 us)
Async XLA Ops:
  2.2 3.6 %copy-start.1 = (bf16[112,64,576]{2,1,0:T(8,128)(2,1)S(1)}, bf16[112,64,576]{2,1,0:T(8,128)(2,1)}, u32[]{:S(2)}) copy-start(bf16[112,64,576]{2,1,0:T(8,128)(2,1)} %pool_ref.3) | copy-start | bytes 24772612
  8.8 2.2 %copy-start = (bf16[32,64,1152]{2,1,0:T(8,128)(2,1)}, bf16[32,64,1152]{2,1,0:T(8,128)(2,1)S(1)}, u32[]{:S(2)}) copy-start(bf16[32,64,1152]{2,1,0:T(8,128)(2,1)S(1)} %pack_pages.1) | copy-start | bytes 14155780
  11.0 9.2 %copy-start.10 = (s32[768]{0:T(1024)S(1)}, s32[768]{0:T(1024)}, u32[]{:S(2)}) copy-start(s32[768]{0:T(1024)} %param.18) | copy-start | bytes 9220
  11.0 9.5 %copy-start.3 = (bf16[16,64,576]{2,1,0:T(8,128)(2,1)S(1)}, bf16[16,64,576]{2,1,0:T(8,128)(2,1)}, u32[]{:S(2)}) copy-start(bf16[16,64,576]{2,1,0:T(8,128)(2,1)} %q_ref.3) | copy-start | bytes 3538948
  11.0 9.5 %copy-start.8 = (s32[16,32]{1,0:T(8,128)S(1)}, s32[16,32]{1,0:T(8,128)}, u32[]{:S(2)}) copy-start(s32[16,32]{1,0:T(8,128)} %table.1) | copy-start | bytes 6148
  11.0 9.5 %copy-start.9 = (s32[16]{0:T(128)S(1)}, s32[16]{0:T(128)}, u32[]{:S(2)}) copy-start(s32[16]{0:T(128)} %lens.1) | copy-start | bytes 196
  11.0 67.5 %all-to-all-start = ((bf16[32,64,1152]{2,1,0:T(8,128)(2,1)}), bf16[32,64,1152]{2,1,0:T(8,128)(2,1)}, u32[]{:S(2)}, u32[]{:S(2)}) async-start(bf16[32,64,1152]{2,1,0:T(8,128)(2,1)} %copy-done), calls=%async_computation | async-start | bytes 9437184 | tf_op jit(solution)/shard_map/all_to_all | solution.py:555
  20.5 3.6 %copy-start.2 = (bf16[112,64,576]{2,1,0:T(8,128)(2,1)S(1)}, bf16[112,64,576]{2,1,0:T(8,128)(2,1)}, u32[]{:S(2)}) copy-start(bf16[112,64,576]{2,1,0:T(8,128)(2,1)} %pool_ref.3) | copy-start | bytes 24772612
  52.7 0.8 copy-start.4
  53.5 0.8 copy-start.6
  78.5 1.0 copy-start.5
  79.5 1.0 copy-start.7

commit v3 on v1

--- a/solution.py
+++ b/solution.py
@@ -30,162 +30,237 @@
     return pl.BlockSpec(memory_space=pl.ANY)
 
 
-def pack_kernel(ids_ref, pool_ref, out_ref, sem):
-    count = out_ref.shape[0]
-
-    def start(i, carry):
-        pltpu.make_async_copy(pool_ref.at[ids_ref[i]], out_ref.at[i], sem).start()
+def attend_kernel(
+    ids, entries, index, slots, rc, table, lens, q_ref, pool_hbm, out_ref,
+    pool, outbox, via, inbox, pages, mult, acc, top, total,
+    pool_sems, copy_sems, one_ss, one_rs, two_ss, two_rs,
+):
+    me = lax.axis_index("dp")
+    core = lax.rem(me, 2)
+    chip = me // 2
+    x = chip // NZ
+    z = lax.rem(chip, NZ)
+    rows, heads, width = q_ref.shape
+    page = pool.shape[1]
+    part = page // 2
+    refs = table.shape[1]
+    moves = slots.shape[0]
+
+    loads = []
+    for k in range(4):
+        span = pl.ds(k * (pool.shape[0] // 4), pool.shape[0] // 4)
+        loads.append(pltpu.make_async_copy(pool_hbm.at[span], pool.at[span], pool_sems.at[k]))
+        loads[-1].start()
+
+    def device(a, b, e):
+        return (lax.rem(x + a, NX) * NZ + lax.rem(z + b, NZ)) * 2 + lax.rem(core + e, 2)
+
+    def on(a, b, e):
+        return {"dp": device(a, b, e)}
+
+    near = [(0, 0, 1)] + [(a, 0, e) for a in (1, 2, 3) for e in (0, 1)] + [(0, b, e) for b in (1, 2, 3) for e in (0, 1)]
+    barrier = pltpu.get_barrier_semaphore()
+    for at in near:
+        pl.semaphore_signal(barrier, inc=1, device_id=on(*at), device_id_type=MESH)
+    pl.semaphore_wait(barrier, len(near))
+    for copy in loads:
+        copy.wait()
+
+    sent = []
+
+    def send(src, dst, ss, rs, to):
+        copy = pltpu.make_async_remote_copy(
+            src_ref=src, dst_ref=dst, send_sem=ss, recv_sem=rs, device_id=to, device_id_type=MESH
+        )
+        copy.start()
+        sent.append(copy)
+        return copy
+
+    def pack(i, first):
+        d = first + i
+        one, two = pool[ids[2 * d]], pool[ids[2 * d + 1]]
+        rope = jnp.concatenate([one[:, LATENT:], two[:, LATENT:]], axis=1)
+        for h in range(2):
+            rs = slice(h * part, (h + 1) * part)
+            outbox[h, d, :, :LATENT] = one[rs, :LATENT]
+            outbox[h, d, :, LATENT : 2 * LATENT] = two[rs, :LATENT]
+            outbox[h, d, :, 2 * LATENT :] = rope[rs]
+        return first
+
+    one_copies = {}
+    final = {}
+    local = []
+
+    def deliver(h, a, b, e, src):
+        origin = (lax.rem(x + (NX - a if h == 0 else 0), NX) * NZ + lax.rem(z + (0 if h == 0 else NZ - b), NZ)) * 2 + core
+        dst = inbox.at[origin, pl.ds(h * part, part), :]
+        at = ((a * NZ + b) * 2 + e) * 2 + h
+        da, db = (0, b) if h == 0 else (a, 0)
+        if (da, db, e) == (0, 0, 0):
+            copy = pltpu.make_async_copy(src, dst, copy_sems.at[len(local)])
+            copy.start()
+            local.append(copy)
+        else:
+            final[at] = send(src, dst, two_ss.at[at], two_rs.at[at], on(da, db, e))
+
+    for n, a in enumerate((2, 1, 3, 0)):
+        xa = lax.rem(x + a, NX)
+        lax.fori_loop(0, 8, pack, xa * 8)
+        if a:
+            one_copies[0, a] = send(
+                outbox.at[0, pl.ds(xa * 8, 8)], via.at[0, a - 1], one_ss.at[a - 1], one_rs.at[a - 1], on(a, 0, 0)
+            )
+        for b in (2, 1, 3):
+            zb = lax.rem(z + b, NZ)
+            at = 3 + (b - 1) * 4 + n
+            one_copies[1, b, n] = send(
+                outbox.at[1, pl.ds(xa * 8 + zb * 2, 2)],
+                via.at[1, b - 1, pl.ds(xa * 2, 2)],
+                one_ss.at[at],
+                one_rs.at[at],
+                on(0, b, 0),
+            )
+
+    def second_hop(k):
+        if k:
+            one_copies[0, k].wait_recv()
+            for n in range(4):
+                one_copies[1, k, n].wait_recv()
+        for o in (2, 1, 3, 0):
+            for e in range(2):
+                ce = lax.rem(core + e, 2)
+                zo, xo = lax.rem(z + o, NZ), lax.rem(x + o, NX)
+                deliver(0, k, o, e, via.at[0, k - 1, zo * 2 + ce] if k else outbox.at[0, x * 8 + zo * 2 + ce])
+                deliver(1, o, k, e, via.at[1, k - 1, xo * 2 + ce] if k else outbox.at[1, xo * 8 + z * 2 + ce])
+
+    def attend_row(r, carry):
+        q = q_ref[r]
+        group = 8
+        col = lax.broadcasted_iota(jnp.int32, (1, page * group), 1)
+        keys, scores = [], []
+        for g in range(refs // group):
+            es = [entries[r * refs + g * group + i] for i in range(group)]
+            k = jnp.concatenate([pool[e >> 7] for e in es], axis=0)
+            limit = jnp.zeros((1, page * group), jnp.int32)
+            for i, e in enumerate(es):
+                limit = jnp.where((col >> 6) == i, e & 127, limit)
+            s = lax.dot_general(q, k, (((1,), (1,)), ((), ())), preferred_element_type=F32) * SOFTMAX_SCALE
+            scores.append(jnp.where((col & 63) < limit, s, LOW))
+            keys.append(k)
+        m = functools.reduce(jnp.maximum, [jnp.max(s, axis=1, keepdims=True) for s in scores])
+        t = jnp.zeros((heads, 1), F32)
+        o = jnp.zeros((heads, LATENT), F32)
+        for s, k in zip(scores, keys):
+            p = jnp.exp(s - m)
+            t = t + jnp.sum(p, axis=1, keepdims=True)
+            o = o + jnp.dot(p.astype(BF16), k[:, :LATENT], preferred_element_type=F32)
+        some = m > 0.5 * LOW
+        acc[r] = jnp.where(some, o, 0.0)
+        top[r] = jnp.broadcast_to(m, (heads, 128))
+        total[r] = jnp.broadcast_to(jnp.where(some, t, 0.0), (heads, 128))
         return carry
 
-    lax.fori_loop(0, count, start, 0)
-    pltpu.make_async_copy(out_ref, out_ref, sem).wait()
-
-
-def pack_pages(ids, pool):
+    second_hop(0)
+    lax.fori_loop(0, 5, attend_row, 0)
+    second_hop(1)
+    second_hop(3)
+    lax.fori_loop(5, 9, attend_row, 0)
+    second_hop(2)
+    lax.fori_loop(9, rows, attend_row, 0)
+
+    row = lax.broadcasted_iota(jnp.int32, (rows, refs), 0)
+    pos = lax.broadcasted_iota(jnp.int32, (rows, refs), 1)
+    valid = jnp.where(row < rc[0], jnp.clip(lens[...] - page * pos, 0, page), 0)
+    whole = (valid == page).astype(F32)
+    some = ((valid > 0) & (valid < page)).astype(F32)
+    last = jnp.sum(some * valid.astype(F32), axis=1, keepdims=True)
+    off = lax.broadcasted_iota(jnp.int32, (rows, page), 1).astype(F32)
+    inside = (off < last).astype(F32)
+    for i in range(0, moves, 2):
+        pair = []
+        for j in (i, i + 1):
+            hit = (table[...] == slots[j]).astype(F32)
+            pair.append(
+                jnp.sum(hit * whole, axis=1, keepdims=True) + jnp.sum(hit * some, axis=1, keepdims=True) * inside
+            )
+        mult[:, i * page : (i + 2) * page] = jnp.concatenate(pair, axis=1)
+
+    for copy in local:
+        copy.wait()
+    for copy in final.values():
+        copy.wait_recv()
+
+    def unpack(i, carry):
+        at = index[i]
+        pair = inbox[at >> 1]
+        first = (at & 1) == 0
+        here = pl.ds(pl.multiple_of(i * page, page), page)
+        rope = width - LATENT
+        pages[here, :LATENT] = jnp.where(first, pair[:, :LATENT], pair[:, LATENT : 2 * LATENT])
+        pages[here, LATENT:] = jnp.where(
+            first, pair[:, 2 * LATENT : 2 * LATENT + rope], pair[:, 2 * LATENT + rope :]
+        )
+        return carry
+
+    lax.fori_loop(0, moves, unpack, 0)
+
+    step = 4
+
+    def moved_rows(n, carry):
+        rs = pl.ds(n * step, step)
+        q = q_ref[rs].reshape(step * heads, width)
+        s = lax.dot_general(q, pages[...], (((1,), (1,)), ((), ())), preferred_element_type=F32) * SOFTMAX_SCALE
+        times = jnp.concatenate(
+            [jnp.broadcast_to(mult[pl.ds(n * step + i, 1), :], (heads, moves * page)) for i in range(step)], axis=0
+        )
+        s = jnp.where(times > 0.0, s, LOW)
+        old = top[rs].reshape(step * heads, 128)[:, :1]
+        m = jnp.maximum(old, jnp.max(s, axis=1, keepdims=True))
+        shrink = jnp.exp(old - m)
+        p = jnp.exp(s - m) * times
+        t = total[rs].reshape(step * heads, 128)[:, :1] * shrink + jnp.sum(p, axis=1, keepdims=True)
+        o = acc[rs].reshape(step * heads, LATENT) * shrink
+        o = o + jnp.dot(p.astype(BF16), pages[:, :LATENT], preferred_element_type=F32)
+        o = o / jnp.where(t == 0.0, 1.0, t)
+        out_ref[rs] = o.astype(BF16).reshape(step, heads, LATENT)
+        return carry
+
+    lax.fori_loop(0, rows // step, moved_rows, 0)
+    while sent:
+        sent.pop().wait_send()
+
+
+def attend(ids, entries, index, slots, rc, table, lens, queries, pool):
+    rows, heads, width = queries.shape
+    count, page, _ = pool.shape
+    moves = slots.shape[0]
+    ranks = NX * NZ * 2
+    dma = pltpu.SemaphoreType.DMA
     return pl.pallas_call(
-        pack_kernel,
-        out_shape=jax.ShapeDtypeStruct((ids.shape[0],) + pool.shape[1:], pool.dtype),
-        in_specs=[sspec(), aspec()],
-        out_specs=aspec(),
-        scratch_shapes=[pltpu.SemaphoreType.DMA],
-        name="pack_pages",
-    )(ids, pool)
-
-
-def flash_step(q, pages_ref, entries, carry):
-    top, total, acc = carry
-    group = len(entries)
-    k = jnp.concatenate([pages_ref[e >> 7] for e in entries], axis=0)
-    s = lax.dot_general(q, k, (((1,), (1,)), ((), ())), preferred_element_type=F32) * SOFTMAX_SCALE
-    col = lax.broadcasted_iota(jnp.int32, (1, 64 * group), 1)
-    limit = jnp.zeros((1, 64 * group), jnp.int32)
-    for g, e in enumerate(entries):
-        limit = jnp.where((col >> 6) == g, e & 127, limit)
-    s = jnp.where((col & 63) < limit, s, LOW)
-    new_top = jnp.maximum(top, jnp.max(s, axis=1, keepdims=True))
-    shrink = jnp.exp(top - new_top)
-    p = jnp.exp(s - new_top)
-    total = total * shrink + jnp.sum(p, axis=1, keepdims=True)
-    acc = acc * shrink + jnp.dot(p.astype(BF16), k[:, :LATENT], preferred_element_type=F32)
-    return new_top, total, acc
-
-
-GROUP_A = 8
-GROUP_B = 4
-LIST = 40
-
-
-def local_kernel(table, lens, rc, slots, q_ref, pool_ref, acc_ref, top_ref, total_ref, list_ref, count_ref, slotmap, list_a):
-    rows, heads = q_ref.shape[0], q_ref.shape[1]
-
-    def clear(i, carry):
-        slotmap[i] = -1
-        return carry
-
-    lax.fori_loop(0, pool_ref.shape[0], clear, 0)
-
-    def mark(i, carry):
-        slotmap[slots[i]] = i
-        return carry
-
-    lax.fori_loop(0, slots.shape[0], mark, 0)
-
-    def row(r, carry):
-        length = lens[r]
-        pages = jnp.where(r < rc[0], (length + 63) // 64, 0)
-
-        def place(p, c):
-            a, b = c
-            slot = table[r, p]
-            valid = jnp.minimum(length - 64 * p, 64)
-            moved = slotmap[slot]
-            list_a[a] = slot * 128 + valid
-            list_ref[r * LIST + b] = moved * 128 + valid
-            is_moved = (moved >= 0).astype(jnp.int32)
-            return a + 1 - is_moved, b + is_moved
-
-        a, b = lax.fori_loop(0, pages, place, (0, 0))
-        for g in range(GROUP_A):
-            list_a[a + g] = 0
-        for g in range(GROUP_B):
-            list_ref[r * LIST + b + g] = 0
-        count_ref[r] = b
-        q = q_ref[r]
-
-        def step(i, c):
-            return flash_step(q, pool_ref, [list_a[i * GROUP_A + g] for g in range(GROUP_A)], c)
-
-        init = (
-            jnp.full((heads, 1), LOW, F32),
-            jnp.zeros((heads, 1), F32),
-            jnp.zeros((heads, LATENT), F32),
-        )
-        top, total, acc = lax.fori_loop(0, (a + GROUP_A - 1) // GROUP_A, step, init)
-        acc_ref[r] = acc
-        top_ref[r] = jnp.broadcast_to(top, (heads, 128))
-        total_ref[r] = jnp.broadcast_to(total, (heads, 128))
-        return carry
-
-    lax.fori_loop(0, rows, row, 0)
-
-
-def attend_local(table, lens, rc, slots, queries, pool):
-    rows, heads, _ = queries.shape
-    return pl.pallas_call(
-        local_kernel,
-        out_shape=(
-            jax.ShapeDtypeStruct((rows, heads, LATENT), F32),
-            jax.ShapeDtypeStruct((rows, heads, 128), F32),
-            jax.ShapeDtypeStruct((rows, heads, 128), F32),
-            jax.ShapeDtypeStruct((rows * LIST,), jnp.int32),
-            jax.ShapeDtypeStruct((rows,), jnp.int32),
-        ),
-        in_specs=[sspec(), sspec(), sspec(), sspec(), vspec(), vspec()],
-        out_specs=(vspec(), vspec(), vspec(), sspec(), sspec()),
-        scratch_shapes=[pltpu.SMEM((pool.shape[0],), jnp.int32), pltpu.SMEM((LIST + 8,), jnp.int32)],
-        compiler_params=pltpu.CompilerParams(vmem_limit_bytes=40 * 2**20),
-        cost_estimate=pl.CostEstimate(flops=20_000_000_000, bytes_accessed=14_000_000, transcendentals=2_000_000),
-        name="attend_local",
-    )(table, lens, rc, slots, queries, pool)
-
-
-def moved_kernel(list_ref, count_ref, index_ref, q_ref, acc_ref, top_ref, total_ref, in_ref, out_ref, pages, sem):
-    rows = q_ref.shape[0]
-    count = pages.shape[0]
-
-    def start(i, carry):
-        pltpu.make_async_copy(in_ref.at[index_ref[i]], pages.at[i], sem).start()
-        return carry
-
-    lax.fori_loop(0, count, start, 0)
-    pltpu.make_async_copy(pages, pages, sem).wait()
-
-    def row(r, carry):
-        q = q_ref[r]
-
-        def step(i, c):
-            return flash_step(q, pages, [list_ref[r * LIST + i * GROUP_B + g] for g in range(GROUP_B)], c)
-
-        init = (top_ref[r][:, :1], total_ref[r][:, :1], acc_ref[r])
-        _, total, acc = lax.fori_loop(0, (count_ref[r] + GROUP_B - 1) // GROUP_B, step, init)
-        total = jnp.where(total == 0.0, 1.0, total)
-        out_ref[r] = (acc / total).astype(BF16)
-        return carry
-
-    lax.fori_loop(0, rows, row, 0)
-
-
-def attend_moved(list_b, count_b, index, queries, acc, top, total, incoming):
-    rows, heads, width = queries.shape
-    return pl.pallas_call(
-        moved_kernel,
+        attend_kernel,
         out_shape=jax.ShapeDtypeStruct((rows, heads, LATENT), BF16),
-        in_specs=[sspec(), sspec(), sspec(), vspec(), vspec(), vspec(), vspec(), aspec()],
+        in_specs=[sspec()] * 5 + [vspec()] * 3 + [aspec()],
         out_specs=vspec(),
-        scratch_shapes=[pltpu.VMEM((index.shape[0], incoming.shape[1], width), BF16), pltpu.SemaphoreType.DMA],
-        compiler_params=pltpu.CompilerParams(vmem_limit_bytes=40 * 2**20),
-        name="attend_moved",
-    )(list_b, count_b, index, queries, acc, top, total, incoming)
+        scratch_shapes=[
+            pltpu.VMEM(pool.shape, BF16),
+            pltpu.VMEM((2, ranks, page // 2, 2 * width), BF16),
+            pltpu.VMEM((2, 3, 8, page // 2, 2 * width), BF16),
+            pltpu.VMEM((ranks, page, 2 * width), BF16),
+            pltpu.VMEM((moves * page, width), BF16),
+            pltpu.VMEM((rows, moves * page), F32),
+            pltpu.VMEM((rows, heads, LATENT), F32),
+            pltpu.VMEM((rows, heads, 128), F32),
+            pltpu.VMEM((rows, heads, 128), F32),
+            dma((4,)),
+            dma((8,)),
+            dma((15,)),
+            dma((15,)),
+            dma((64,)),
+            dma((64,)),
+        ],
+        compiler_params=pltpu.CompilerParams(collective_id=1, has_side_effects=True, vmem_limit_bytes=VMEM_LIMIT),
+        name="attend",
+    )(ids, entries, index, slots, rc, table, lens.reshape(rows, 1), queries, pool)
 
 
 SUBS = 2
@@ -537,18 +612,18 @@
         arrival[:, :, None] == jnp.arange(capacity)[None, None, :]
     )
     send_ids = jnp.sum(jnp.where(chosen, page_ids[:, :, None], 0), axis=1).reshape(-1)
-    page_shape = page_pool.shape[1:]
-    outgoing = pack_pages(send_ids, page_pool).reshape((rank_count, capacity) + page_shape)
-    incoming = lax.all_to_all(outgoing, "dp", split_axis=0, concat_axis=0, tiled=True)
     own_sources = lax.dynamic_index_in_dim(sources, own_rank, 0, keepdims=False)
     own_arrival = lax.dynamic_index_in_dim(arrival, own_rank, 0, keepdims=False)
     own_slots = lax.dynamic_index_in_dim(slot_ids, own_rank, 0, keepdims=False)
-    acc, top, total, list_b, count_b = attend_local(
-        page_table, lengths, row_count, own_slots, queries, page_pool
-    )
-    latent = attend_moved(
-        list_b, count_b, own_sources * capacity + own_arrival, queries, acc, top, total,
-        incoming.reshape((rank_count * capacity,) + page_shape),
+    rows, refs = page_table.shape
+    page = page_pool.shape[1]
+    valid = jnp.clip(lengths[:, None] - page * jnp.arange(refs)[None, :], 0, page)
+    valid = jnp.where((jnp.arange(rows) < row_count[0])[:, None], valid, 0)
+    is_moved = jnp.any(page_table[:, :, None] == own_slots[None, None, :], axis=2)
+    entries = jnp.where(is_moved, 0, page_table * 128 + valid).reshape(-1)
+    latent = attend(
+        send_ids, entries, own_sources * capacity + own_arrival, own_slots, row_count, page_table, lengths,
+        queries, page_pool,
     )
     rows, heads, _ = latent.shape
     lat = latent.reshape(rows, NX * NZ, heads // (NX * NZ), LATENT).transpose(1, 2, 0, 3)

time: 363 us -> 189 us (0.52)
  Pallas kernels: 285 us -> 175 us
  waiting for transfers between devices: 54.6 us -> 0 us
  starting transfers between devices: 8.51 us -> 0 us
    pallas_call x3 -> x1, Pallas kernels: 169 us -> 72.2 us  [attend(): pl.pallas_call(attend_kernel, out_shape=jax.ShapeDtypeStruct((rows, heads...]
    all_to_all x1 -> x0, waiting for transfers between devices: 54.6 us -> none  [body(): lax.all_to_all(outgoing, 'dp', split_axis=0, concat_axis=0, tiled=True)]
    pallas_call x1, Pallas kernels: 116 us -> 103 us  [tail(): pl.pallas_call(tail_kernel, out_shape=jax.ShapeDtypeStruct(residual.shape...]
    all_to_all x1 -> x0, starting transfers between devices: 8.51 us -> none  [body(): lax.all_to_all(outgoing, 'dp', split_axis=0, concat_axis=0, tiled=True)]
    unnamed x19 -> x3, local copies, waits for them, and re-layouts: 8.98 us -> 1.65 us
  transfers between devices with their start and end apart: 1 -> 0, of which waited for: 1 -> 0; matrix products, arithmetic and copies ran while one was open for 0% -> 0% of each run, Pallas kernels for 1% -> 0%
where the time goes in v3:
time: 189 us; the launch traced here: 188 us
  Pallas kernels  175 us (93%)
  local copies, waits for them, and re-layouts  9.04 us (5%)
  other arithmetic  3.27 us (2%)
    pallas_call x1, Pallas kernels, tail(): pl.pallas_call(tail_kernel, out_shape=jax.ShapeDtypeStruct(residual.shape...  103 us
    pallas_call x1, Pallas kernels, attend(): pl.pallas_call(attend_kernel, out_shape=jax.ShapeDtypeStruct((rows, heads...  72.2 us

profile of v3, /device:TPU:0, one launch (start us, length us, event | category | flops | bytes accessed | tf_op | source)
XLA Modules:
  0.0 187.8 jit_solution(2007122660660719490)
XLA Ops:
  0.7 0.7 reduce
  1.4 1.3 copy.34.lens
  2.7 0.1 reshape.62
  2.8 0.1 copy.29
  2.9 0.1 copy.28
  3.0 0.2 convert_reduce_fusion
  3.2 0.8 add_reduce_fusion.index
  3.9 0.8 broadcast_in_dim.40
  4.7 0.1 copy.31
  4.8 0.1 copy.32
  4.9 0.6 reshape.63.ids
  5.5 0.8 reshape.64
  6.3 0.0 copy-start
  6.3 0.8 compare_reduce_fusion
  7.1 0.8 add_select_fusion
  7.9 0.7 reshape.65.entries
  8.6 0.0 copy-done
  8.6 72.2 %attend.1 = bf16[16,64,512]{2,1,0:T(8,128)(2,1)} custom-call(s32[64]{0:T(128)} %reshape.63.ids, s32[512]{0:T(512)} %reshape.65.entries, s32[24]{0:T(128)} %add_reduce_fusion.index, s32[24]{0:T(128)} %copy-done, s32[1]{0:T(128)} %copy.38.rc, s32[16,32]{1,0:T(8,128)} %table.1, s32[16,1]{1,0:T(8,128)} %copy.34.lens, bf16[16,64,576]{2,1,0:T(8,128)(2,1)} %q_ref.1, ...), custom_call_target="tpu_custom_call" | custom-call | tf_op jit(solution)/shard_map/attend/pallas_call | solution.py:239
  80.7 2.8 %copy.36 = bf16[16,64,512]{2,0,1:T(8,128)(2,1)} copy(bf16[16,64,512]{2,1,0:T(8,128)(2,1)} %attend.1) | data formatting | bytes 2097152 | tf_op jit(solution)/shard_map/reshape | solution.py:629
  83.6 102.6 %tail.1 = bf16[16,7168]{1,0:T(8,128)(2,1)} custom-call(bf16[16,64,512]{2,1,0:T(8,128)(2,1)} %bitcast.13, bf16[2,512,128]{2,1,0:T(8,128)(2,1)} %vu.1, bf16[256,7168]{1,0:T(8,128)(2,1)} %wo.1, bf16[16,7168]{1,0:T(8,128)(2,1)} %res.1, f32[1,7168]{1,0:T(1,128)} %bitcast.17, bf16[288,7168]{1,0:T(8,128)(2,1)} %bitcast.15, bf16[288,7168]{1,0:T(8,128)(2,1)} %bitcast.16, ...), custom_call_target="tpu_custom_call" | custom-call | flops 12000000000 | bytes 40000000 | tf_op jit(solution)/shard_map/tail/pallas_call | solution.py:546
  186.2 1.6 copy.39
  (6 shorter events, 0.1 us)
Async XLA Ops:
  6.3 2.3 %copy-start = (s32[24]{0:T(128)}, s32[24]{0:T(128)S(1)}, u32[]{:S(2)}) copy-start(s32[24]{0:T(128)S(1)} %fusion.1.slots) | copy-start | bytes 292

commit v4 on v3

--- a/solution.py
+++ b/solution.py
@@ -31,9 +31,9 @@
 
 
 def attend_kernel(
-    ids, entries, index, slots, rc, table, lens, q_ref, pool_hbm, out_ref,
-    pool, outbox, via, inbox, pages, mult, acc, top, total,
-    pool_sems, copy_sems, one_ss, one_rs, two_ss, two_rs,
+    src, page_of, slot_of, rc, lens, table, q_ref, pool_hbm, vu, wo, out_ref, vu_out, wo_out,
+    pool, outbox, via, inbox, pages, mult, acc, top, total, packed, vu_box, wo_box, entries_v, entries,
+    pool_sems, copy_sems, one_ss, one_rs, two_ss, two_rs, w_ss, w_rs, lat_ss, lat_rs,
 ):
     me = lax.axis_index("dp")
     core = lax.rem(me, 2)
@@ -44,7 +44,8 @@
     page = pool.shape[1]
     part = page // 2
     refs = table.shape[1]
-    moves = slots.shape[0]
+    moves = pages.shape[0] // page
+    mine = me * moves
 
     loads = []
     for k in range(4):
@@ -59,10 +60,24 @@
         return {"dp": device(a, b, e)}
 
     near = [(0, 0, 1)] + [(a, 0, e) for a in (1, 2, 3) for e in (0, 1)] + [(0, b, e) for b in (1, 2, 3) for e in (0, 1)]
+    far = [(a, b, 0) for a in (1, 2, 3) for b in (1, 2, 3)]
     barrier = pltpu.get_barrier_semaphore()
-    for at in near:
+    for at in near + far:
         pl.semaphore_signal(barrier, inc=1, device_id=on(*at), device_id_type=MESH)
-    pl.semaphore_wait(barrier, len(near))
+
+    row = lax.broadcasted_iota(jnp.int32, (rows, refs), 0)
+    pos = lax.broadcasted_iota(jnp.int32, (rows, refs), 1)
+    length = jnp.zeros((rows, refs), jnp.int32)
+    for r in range(rows):
+        length = jnp.where(row == r, jnp.where(r < rc[0], lens[r], 0), length)
+    valid = jnp.clip(length - page * pos, 0, page)
+    entry = table[...] * 128 + valid
+    for i in range(moves):
+        entry = jnp.where(table[...] == slot_of[mine + i], 0, entry)
+    entries_v[:, :refs] = entry
+    to_scalar = pltpu.make_async_copy(entries_v, entries, pool_sems.at[4])
+    to_scalar.start()
+    pl.semaphore_wait(barrier, len(near + far))
     for copy in loads:
         copy.wait()
 
@@ -78,7 +93,13 @@
 
     def pack(i, first):
         d = first + i
-        one, two = pool[ids[2 * d]], pool[ids[2 * d + 1]]
+        hits = [src[0, d * moves + j] == me for j in range(moves)]
+        named = [page_of[d * moves + j] for j in range(moves)]
+        early, late = 0, 0
+        for j in range(moves):
+            late = jnp.where(hits[j], named[j], late)
+            early = jnp.where(hits[moves - 1 - j], named[moves - 1 - j], early)
+        one, two = pool[early], pool[late]
         rope = jnp.concatenate([one[:, LATENT:], two[:, LATENT:]], axis=1)
         for h in range(2):
             rs = slice(h * part, (h + 1) * part)
@@ -139,7 +160,7 @@
         col = lax.broadcasted_iota(jnp.int32, (1, page * group), 1)
         keys, scores = [], []
         for g in range(refs // group):
-            es = [entries[r * refs + g * group + i] for i in range(group)]
+            es = [entries[r, g * group + i] for i in range(group)]
             k = jnp.concatenate([pool[e >> 7] for e in es], axis=0)
             limit = jnp.zeros((1, page * group), jnp.int32)
             for i, e in enumerate(es):
@@ -160,7 +181,12 @@
         total[r] = jnp.broadcast_to(jnp.where(some, t, 0.0), (heads, 128))
         return carry
 
+    w_copies = [
+        send(vu, vu_box, w_ss.at[0], w_rs.at[0], on(0, 0, 1)),
+        send(wo, wo_box, w_ss.at[1], w_rs.at[1], on(0, 0, 1)),
+    ]
     second_hop(0)
+    to_scalar.wait()
     lax.fori_loop(0, 5, attend_row, 0)
     second_hop(1)
     second_hop(3)
@@ -168,9 +194,12 @@
     second_hop(2)
     lax.fori_loop(9, rows, attend_row, 0)
 
-    row = lax.broadcasted_iota(jnp.int32, (rows, refs), 0)
-    pos = lax.broadcasted_iota(jnp.int32, (rows, refs), 1)
-    valid = jnp.where(row < rc[0], jnp.clip(lens[...] - page * pos, 0, page), 0)
+    for k, (box, out) in enumerate(((vu_box, vu_out), (wo_box, wo_out))):
+        w_copies[k].wait_recv()
+        w_copies[k] = pltpu.make_async_copy(box, out, pool_sems.at[k])
+        w_copies[k].start()
+
+    block = 16
     whole = (valid == page).astype(F32)
     some = ((valid > 0) & (valid < page)).astype(F32)
     last = jnp.sum(some * valid.astype(F32), axis=1, keepdims=True)
@@ -179,98 +208,130 @@
     for i in range(0, moves, 2):
         pair = []
         for j in (i, i + 1):
-            hit = (table[...] == slots[j]).astype(F32)
+            hit = (table[...] == slot_of[mine + j]).astype(F32)
             pair.append(
                 jnp.sum(hit * whole, axis=1, keepdims=True) + jnp.sum(hit * some, axis=1, keepdims=True) * inside
             )
-        mult[:, i * page : (i + 2) * page] = jnp.concatenate(pair, axis=1)
+        pair = jnp.concatenate(pair, axis=1)
+        for r in range(rows):
+            mult[r * block : (r + 1) * block, i * page : (i + 2) * page] = jnp.broadcast_to(
+                pair[r : r + 1], (block, 2 * page)
+            )
+
+    places = []
+    for i in range(moves):
+        again = 0
+        for j in range(i):
+            again = again + (src[0, mine + i] == src[0, mine + j]).astype(jnp.int32)
+        places.append((src[0, mine + i], again))
 
     for copy in local:
         copy.wait()
     for copy in final.values():
         copy.wait_recv()
 
-    def unpack(i, carry):
-        at = index[i]
-        pair = inbox[at >> 1]
-        first = (at & 1) == 0
-        here = pl.ds(pl.multiple_of(i * page, page), page)
-        rope = width - LATENT
+    rope = width - LATENT
+    for i, (rank, again) in enumerate(places):
+        pair = inbox[rank]
+        first = again == 0
+        here = slice(i * page, (i + 1) * page)
         pages[here, :LATENT] = jnp.where(first, pair[:, :LATENT], pair[:, LATENT : 2 * LATENT])
         pages[here, LATENT:] = jnp.where(
             first, pair[:, 2 * LATENT : 2 * LATENT + rope], pair[:, 2 * LATENT + rope :]
         )
-        return carry
-
-    lax.fori_loop(0, moves, unpack, 0)
-
-    step = 4
-
-    def moved_rows(n, carry):
-        rs = pl.ds(n * step, step)
-        q = q_ref[rs].reshape(step * heads, width)
+
+    size = rows * block
+    to = lax.broadcasted_iota(jnp.int32, (size, size), 0)
+    frm = lax.broadcasted_iota(jnp.int32, (size, size), 1)
+    turn = (frm == (to % rows) * block + to // rows).astype(BF16)
+    lat_copies = []
+    for n, a in enumerate((2, 1, 3, 0)):
+        xa = lax.rem(x + a, NX)
+        hs = pl.ds(pl.multiple_of(xa * block, block), block)
+        q = q_ref[:, hs, :].reshape(size, width)
         s = lax.dot_general(q, pages[...], (((1,), (1,)), ((), ())), preferred_element_type=F32) * SOFTMAX_SCALE
-        times = jnp.concatenate(
-            [jnp.broadcast_to(mult[pl.ds(n * step + i, 1), :], (heads, moves * page)) for i in range(step)], axis=0
-        )
+        times = mult[...]
         s = jnp.where(times > 0.0, s, LOW)
-        old = top[rs].reshape(step * heads, 128)[:, :1]
+        old = top[:, hs, :].reshape(size, 128)[:, :1]
         m = jnp.maximum(old, jnp.max(s, axis=1, keepdims=True))
         shrink = jnp.exp(old - m)
         p = jnp.exp(s - m) * times
-        t = total[rs].reshape(step * heads, 128)[:, :1] * shrink + jnp.sum(p, axis=1, keepdims=True)
-        o = acc[rs].reshape(step * heads, LATENT) * shrink
+        t = total[:, hs, :].reshape(size, 128)[:, :1] * shrink + jnp.sum(p, axis=1, keepdims=True)
+        o = acc[:, hs, :].reshape(size, LATENT) * shrink
         o = o + jnp.dot(p.astype(BF16), pages[:, :LATENT], preferred_element_type=F32)
-        o = o / jnp.where(t == 0.0, 1.0, t)
-        out_ref[rs] = o.astype(BF16).reshape(step, heads, LATENT)
-        return carry
-
-    lax.fori_loop(0, rows // step, moved_rows, 0)
+        o = (o / jnp.where(t == 0.0, 1.0, t)).astype(BF16)
+        o = jnp.dot(turn, o, preferred_element_type=F32).astype(BF16)
+        packed[n] = o.reshape(NZ, -1, LATENT)
+        for b in (2, 1, 3, 0):
+            one, dst = packed.at[n, lax.rem(z + b, NZ)], out_ref.at[chip]
+            if (a, b) == (0, 0):
+                own_lat = pltpu.make_async_copy(one, dst, pool_sems.at[2])
+                own_lat.start()
+            else:
+                lat_copies.append(send(one, dst, lat_ss.at[n * 4 + b], lat_rs.at[n * 4 + b], on(a, b, 0)))
+    own_lat.wait()
+    for copy in lat_copies:
+        copy.wait_recv()
+    for copy in w_copies:
+        copy.wait()
     while sent:
         sent.pop().wait_send()
 
 
-def attend(ids, entries, index, slots, rc, table, lens, queries, pool):
+def attend(src, page_of, slot_of, rc, lens, table, queries, pool, value_up, out_proj):
     rows, heads, width = queries.shape
     count, page, _ = pool.shape
-    moves = slots.shape[0]
     ranks = NX * NZ * 2
+    moves = page_of.shape[0] // ranks
     dma = pltpu.SemaphoreType.DMA
     return pl.pallas_call(
         attend_kernel,
-        out_shape=jax.ShapeDtypeStruct((rows, heads, LATENT), BF16),
-        in_specs=[sspec()] * 5 + [vspec()] * 3 + [aspec()],
-        out_specs=vspec(),
+        out_shape=(
+            jax.ShapeDtypeStruct((NX * NZ, rows * heads // (NX * NZ), LATENT), BF16),
+            jax.ShapeDtypeStruct(value_up.shape, BF16),
+            jax.ShapeDtypeStruct(out_proj.shape, BF16),
+        ),
+        in_specs=[sspec()] * 5 + [vspec()] * 2 + [aspec()] * 3,
+        out_specs=(aspec(), aspec(), aspec()),
         scratch_shapes=[
             pltpu.VMEM(pool.shape, BF16),
             pltpu.VMEM((2, ranks, page // 2, 2 * width), BF16),
             pltpu.VMEM((2, 3, 8, page // 2, 2 * width), BF16),
             pltpu.VMEM((ranks, page, 2 * width), BF16),
             pltpu.VMEM((moves * page, width), BF16),
-            pltpu.VMEM((rows, moves * page), F32),
+            pltpu.VMEM((rows * 16, moves * page), F32),
             pltpu.VMEM((rows, heads, LATENT), F32),
             pltpu.VMEM((rows, heads, 128), F32),
             pltpu.VMEM((rows, heads, 128), F32),
-            dma((4,)),
+            pltpu.VMEM((4, NZ, rows * heads // (NX * NZ), LATENT), BF16),
+            pltpu.VMEM(value_up.shape, BF16),
+            pltpu.VMEM(out_proj.shape, BF16),
+            pltpu.VMEM((rows, 128), jnp.int32),
+            pltpu.SMEM((rows, 128), jnp.int32),
+            dma((5,)),
             dma((8,)),
             dma((15,)),
             dma((15,)),
             dma((64,)),
             dma((64,)),
+            dma((2,)),
+            dma((2,)),
+            dma((16,)),
+            dma((16,)),
         ],
         compiler_params=pltpu.CompilerParams(collective_id=1, has_side_effects=True, vmem_limit_bytes=VMEM_LIMIT),
         name="attend",
-    )(ids, entries, index, slots, rc, table, lens.reshape(rows, 1), queries, pool)
+    )(src, page_of, slot_of, rc, lens, table, queries, pool, value_up, out_proj)
 
 
 SUBS = 2
 
 
 def tail_kernel(
-    lat, vu, wo, res, gain, gate, up, down, out_ref,
+    lat, vu, vu2, wo, wo2, res, gain, gate, up, down, out_ref,
     rl, vus, wos, gus, ds, ho, part, nrm, mid, acc, hid,
     b1, b2, c1, c2, e1, e2, f1, f2,
-    bar_sems, lat_ss, lat_rs, w_ls, w_ss, w_rs, rs_ss, rs_rs, ag_ss, ag_rs,
+    in_sems, w_ls, w_ss, w_rs, rs_ss, rs_rs, ag_ss, ag_rs,
 ):
     me = lax.axis_index("dp")
     core = lax.rem(me, 2)
@@ -286,8 +347,22 @@
 
     sibling = {"dp": me + 1 - 2 * core}
 
+    loads = [
+        pltpu.make_async_copy(src, dst, in_sems.at[k])
+        for k, (src, dst) in enumerate(
+            (
+                (lat, rl),
+                (vu, vus.at[core]),
+                (vu2, vus.at[1 - core]),
+                (wo, wos.at[core]),
+                (wo2, wos.at[1 - core]),
+            )
+        )
+    ]
+    for copy in loads:
+        copy.start()
     barrier = pltpu.get_barrier_semaphore()
-    peers = [(a, b) for a in range(NX) for b in range(NZ) if (a, b) != (0, 0)]
+    peers = [(1, 0), (-1, 0), (0, 1), (0, -1)]
     for a, b in peers:
         pl.semaphore_signal(barrier, inc=1, device_id=device(a, b), device_id_type=MESH)
     pl.semaphore_signal(barrier, inc=1, device_id=sibling, device_id_type=MESH)
@@ -303,40 +378,30 @@
         sent.append(copy)
         return copy
 
-    lat_copies = []
-    for k, (a, b) in enumerate(peers):
-        to_chip = lax.rem(x + a, NX) * NZ + lax.rem(z + b, NZ)
-        lat_copies.append(send(lat.at[to_chip], rl.at[chip], lat_ss.at[k], lat_rs.at[k], device(a, b)))
-    own_lat = pltpu.make_async_copy(lat.at[chip], rl.at[chip], bar_sems.at[0])
-    own_lat.start()
-
     row0 = pl.multiple_of(core * ff, 16)
     row1 = pl.multiple_of(640 + core * ff, 16)
     places = [
-        (vu, vus.at[core]),
-        (wo, wos.at[core]),
         (gate, gus.at[pl.ds(row0, ff), :]),
         (up, gus.at[pl.ds(row1, ff), :]),
         (down, ds.at[pl.ds(row0, ff), :]),
     ]
     w_local, w_remote = [], []
-    for k, (src, dst) in enumerate(places):
-        copy = pltpu.make_async_copy(src, dst, w_ls.at[k])
-        copy.start()
-        w_local.append(copy)
-        w_remote.append(send(src, dst, w_ss.at[k], w_rs.at[k], sibling))
-    gus[pl.ds(2 * ff, 640 - 2 * ff), :] = jnp.zeros((640 - 2 * ff, cols_all), BF16)
-    gus[pl.ds(640 + 2 * ff, 640 - 2 * ff), :] = jnp.zeros((640 - 2 * ff, cols_all), BF16)
+
+    def start_weights():
+        for k, (src, dst) in enumerate(places):
+            copy = pltpu.make_async_copy(src, dst, w_ls.at[k])
+            copy.start()
+            w_local.append(copy)
+            w_remote.append(send(src, dst, w_ss.at[k], w_rs.at[k], sibling))
 
     def weights_ready(*ks):
         for k in ks:
             w_local[k].wait()
             w_remote[k].wait_recv()
 
-    own_lat.wait()
-    for copy in lat_copies:
-        copy.wait_recv()
-    weights_ready(0)
+    loads[0].wait()
+    loads[1].wait()
+    loads[2].wait()
     for h in range(4):
         l = rl[:, h * 16 : (h + 1) * 16, :].reshape(256, LATENT)
         ho[:, h * 128 : (h + 1) * 128] = jnp.dot(l, vus[h // 2, h % 2], preferred_element_type=F32).astype(BF16)
@@ -407,6 +472,10 @@
         for h, s in order:
             fill(h * half + s * width, width)
             start(h, s, 0)
+        if turn == 0:
+            start_weights()
+            gus[pl.ds(2 * ff, 640 - 2 * ff), :] = jnp.zeros((640 - 2 * ff, cols_all), BF16)
+            gus[pl.ds(640 + 2 * ff, 640 - 2 * ff), :] = jnp.zeros((640 - 2 * ff, cols_all), BF16)
         for h, s in order:
             middle(h, s, 0)
         for h, s in order:
@@ -417,7 +486,8 @@
         for h, s in order:
             total(h, s, 1)
 
-    weights_ready(1)
+    loads[3].wait()
+    loads[4].wait()
 
     def fill_out(base, size):
         cs = pl.ds(base, size)
@@ -493,7 +563,7 @@
             two[h, n][2].wait_recv()
             two[h, n][3].wait_recv()
 
-    weights_ready(2, 3)
+    weights_ready(0, 1)
     depth = cols_all // 4
 
     def up_step(k, carry):
@@ -515,7 +585,7 @@
     lax.fori_loop(0, 4, up_step, 0)
     g = acc[:, :640]
     hid[...] = (g / (1.0 + jnp.exp(-g)) * acc[:, 640:]).astype(BF16)
-    weights_ready(4)
+    weights_ready(2)
 
     def fill_down(base, size):
         cs = pl.ds(base, size)
@@ -531,7 +601,7 @@
         sent.pop().wait_send()
 
 
-def tail(lat, value_up, out_proj, residual, norm_gain, gate_t, up_t, down):
+def tail(lat, value_up, value_up_2, out_proj, out_proj_2, residual, norm_gain, gate_t, up_t, down):
     cols = residual.shape[1]
     ff = gate_t.shape[0]
     width = cols // 2 // SUBS
@@ -546,7 +616,7 @@
     return pl.pallas_call(
         tail_kernel,
         out_shape=jax.ShapeDtypeStruct(residual.shape, BF16),
-        in_specs=[aspec(), aspec(), aspec(), vspec(), vspec(), aspec(), aspec(), aspec()],
+        in_specs=[aspec()] * 5 + [vspec()] * 2 + [aspec()] * 3,
         out_specs=vspec(),
         scratch_shapes=[
             pltpu.VMEM((16, 64, LATENT), BF16),
@@ -562,12 +632,10 @@
             pltpu.VMEM((256, 640), BF16),
             *rs_bufs,
             *rs_bufs,
-            dma((1,)),
-            dma((15,)),
-            dma((15,)),
             dma((5,)),
-            dma((5,)),
-            dma((5,)),
+            dma((3,)),
+            dma((3,)),
+            dma((3,)),
             dma((n_rs,)),
             dma((n_rs,)),
             dma((40,)),
@@ -576,7 +644,7 @@
         compiler_params=pltpu.CompilerParams(collective_id=0, has_side_effects=True, vmem_limit_bytes=VMEM_LIMIT),
         cost_estimate=pl.CostEstimate(flops=12_000_000_000, bytes_accessed=40_000_000, transcendentals=200_000),
         name="tail",
-    )(lat, value_up, out_proj, residual, norm_gain.reshape(1, cols), gate_t, up_t, down)
+    )(lat, value_up, value_up_2, out_proj, out_proj_2, residual, norm_gain.reshape(1, cols), gate_t, up_t, down)
 
 
 def body(
@@ -596,39 +664,13 @@
     up_proj,
     down_proj,
 ):
-    rank_count = lax.axis_size("dp")
-    own_rank = lax.axis_index("dp")
-    move_count = move_page.shape[0] // rank_count
-    capacity = 2
-    sources = move_source.reshape(rank_count, move_count)
-    page_ids = move_page.reshape(rank_count, move_count)
-    slot_ids = move_slot.reshape(rank_count, move_count)
-    move_order = jnp.arange(move_count)
-    earlier = (sources[:, :, None] == sources[:, None, :]) & (
-        move_order[None, None, :] < move_order[None, :, None]
+    lat, value_up_2, out_proj_2 = attend(
+        move_source.reshape(1, -1), move_page, move_slot, row_count, lengths, page_table, queries, page_pool,
+        value_up, out_proj,
     )
-    arrival = jnp.sum(earlier.astype(jnp.int32), axis=2)
-    chosen = (sources == own_rank)[:, :, None] & (
-        arrival[:, :, None] == jnp.arange(capacity)[None, None, :]
+    return tail(
+        lat, value_up, value_up_2, out_proj, out_proj_2, residual, norm_gain, gate_proj.T, up_proj.T, down_proj
     )
-    send_ids = jnp.sum(jnp.where(chosen, page_ids[:, :, None], 0), axis=1).reshape(-1)
-    own_sources = lax.dynamic_index_in_dim(sources, own_rank, 0, keepdims=False)
-    own_arrival = lax.dynamic_index_in_dim(arrival, own_rank, 0, keepdims=False)
-    own_slots = lax.dynamic_index_in_dim(slot_ids, own_rank, 0, keepdims=False)
-    rows, refs = page_table.shape
-    page = page_pool.shape[1]
-    valid = jnp.clip(lengths[:, None] - page * jnp.arange(refs)[None, :], 0, page)
-    valid = jnp.where((jnp.arange(rows) < row_count[0])[:, None], valid, 0)
-    is_moved = jnp.any(page_table[:, :, None] == own_slots[None, None, :], axis=2)
-    entries = jnp.where(is_moved, 0, page_table * 128 + valid).reshape(-1)
-    latent = attend(
-        send_ids, entries, own_sources * capacity + own_arrival, own_slots, row_count, page_table, lengths,
-        queries, page_pool,
-    )
-    rows, heads, _ = latent.shape
-    lat = latent.reshape(rows, NX * NZ, heads // (NX * NZ), LATENT).transpose(1, 2, 0, 3)
-    lat = lat.reshape(NX * NZ, -1, LATENT)
-    return tail(lat, value_up, out_proj, residual, norm_gain, gate_proj.T, up_proj.T, down_proj)
 
 
 def solution(mesh):

time: 189 us -> 171 us (0.905)
  local copies, waits for them, and re-layouts: 9.04 us -> 1.64 us
  Pallas kernels: 175 us -> 169 us
  other arithmetic: 3.27 us -> 0 us
    pallas_call x1, Pallas kernels: 103 us -> 85.8 us  [tail(): pl.pallas_call(tail_kernel, out_shape=jax.ShapeDtypeStruct(residual.shape...]
    pallas_call x1, Pallas kernels: 72.2 us -> 83 us  [attend(): pl.pallas_call(attend_kernel, out_shape=(jax.ShapeDtypeStruct((NX * NZ, r...]
    reshape x6 -> x0, local copies, waits for them, and re-layouts: 5.04 us -> none  [the longest x1 2.84 us: body(): latent.reshape(rows, NX * NZ, heads // (NX * NZ), LATENT)]
    broadcast_in_dim x3 -> x0, local copies, waits for them, and re-layouts: 2.16 us -> none  [the longest x1 1.33 us: body(): lengths[:, None] - page * jnp.arange(refs)[None, :]]
where the time goes in v4:
time: 171 us
  Pallas kernels  169 us (99%)
    pallas_call x1, Pallas kernels, tail(): pl.pallas_call(tail_kernel, out_shape=jax.ShapeDtypeStruct(residual.shape...  85.8 us
    pallas_call x1, Pallas kernels, attend(): pl.pallas_call(attend_kernel, out_shape=(jax.ShapeDtypeStruct((NX * NZ, r...  83 us

profile of v4, /device:TPU:0, one launch (start us, length us, event | category | flops | bytes accessed | tf_op | source)
XLA Modules:
  0.0 171.2 jit_solution(6340861297704967301)
XLA Ops:
  0.7 83.0 %attend.1 = (bf16[16,64,512]{2,1,0:T(8,128)(2,1)}, bf16[2,512,128]{2,1,0:T(8,128)(2,1)}, bf16[256,7168]{1,0:T(8,128)(2,1)}) custom-call(s32[1,768]{1,0:T(1,128)} %bitcast.4, s32[768]{0:T(1024)} %page_of.1, s32[768]{0:T(1024)} %slot_of.1, s32[1]{0:T(128)S(6)} %copy.17.rc, s32[16]{0:T(128)} %lens.1, s32[16,32]{1,0:T(8,128)} %table.1, ...), custom_call_target="tpu_custom_call" | custom-call | tf_op jit(solution)/shard_map/attend/pallas_call | solution.py:287
  83.7 85.8 %tail.1 = bf16[16,7168]{1,0:T(8,128)(2,1)} custom-call(bf16[16,64,512]{2,1,0:T(8,128)(2,1)} %get-tuple-element.8.lat, bf16[2,512,128]{2,1,0:T(8,128)(2,1)} %vu.3, bf16[2,512,128]{2,1,0:T(8,128)(2,1)} %get-tuple-element.9.vu2, bf16[256,7168]{1,0:T(8,128)(2,1)} %wo.3, bf16[256,7168]{1,0:T(8,128)(2,1)} %get-tuple-element.10.wo2, bf16[16,7168]{1,0:T(8,128)(2,1)} %res.1, ...), custom_call_target="tpu_custom_call" | custom-call | flops 12000000000 | bytes 40000000 | tf_op jit(solution)/shard_map/tail/pallas_call | solution.py:616
  169.5 1.6 copy.18

commit v5 on v4

--- a/solution.py
+++ b/solution.py
@@ -48,8 +48,8 @@
     mine = me * moves
 
     loads = []
-    for k in range(4):
-        span = pl.ds(k * (pool.shape[0] // 4), pool.shape[0] // 4)
+    for k in range(8):
+        span = pl.ds(k * (pool.shape[0] // 8), pool.shape[0] // 8)
         loads.append(pltpu.make_async_copy(pool_hbm.at[span], pool.at[span], pool_sems.at[k]))
         loads[-1].start()
 
@@ -75,7 +75,7 @@
     for i in range(moves):
         entry = jnp.where(table[...] == slot_of[mine + i], 0, entry)
     entries_v[:, :refs] = entry
-    to_scalar = pltpu.make_async_copy(entries_v, entries, pool_sems.at[4])
+    to_scalar = pltpu.make_async_copy(entries_v, entries, pool_sems.at[8])
     to_scalar.start()
     pl.semaphore_wait(barrier, len(near + far))
     for copy in loads:
@@ -245,7 +245,7 @@
     frm = lax.broadcasted_iota(jnp.int32, (size, size), 1)
     turn = (frm == (to % rows) * block + to // rows).astype(BF16)
     lat_copies = []
-    for n, a in enumerate((2, 1, 3, 0)):
+    for n, a in enumerate((2, 0, 1, 3)):
         xa = lax.rem(x + a, NX)
         hs = pl.ds(pl.multiple_of(xa * block, block), block)
         q = q_ref[:, hs, :].reshape(size, width)
@@ -308,7 +308,7 @@
             pltpu.VMEM(out_proj.shape, BF16),
             pltpu.VMEM((rows, 128), jnp.int32),
             pltpu.SMEM((rows, 128), jnp.int32),
-            dma((5,)),
+            dma((9,)),
             dma((8,)),
             dma((15,)),
             dma((15,)),
@@ -347,26 +347,22 @@
 
     sibling = {"dp": me + 1 - 2 * core}
 
-    loads = [
-        pltpu.make_async_copy(src, dst, in_sems.at[k])
-        for k, (src, dst) in enumerate(
-            (
-                (lat, rl),
-                (vu, vus.at[core]),
-                (vu2, vus.at[1 - core]),
-                (wo, wos.at[core]),
-                (wo2, wos.at[1 - core]),
-            )
-        )
-    ]
-    for copy in loads:
-        copy.start()
+    width = half // SUBS
+    wing = width // 2
+    order = [(h, s) for s in range(SUBS) for h in range(2)]
+
     barrier = pltpu.get_barrier_semaphore()
     peers = [(1, 0), (-1, 0), (0, 1), (0, -1)]
     for a, b in peers:
         pl.semaphore_signal(barrier, inc=1, device_id=device(a, b), device_id_type=MESH)
     pl.semaphore_signal(barrier, inc=1, device_id=sibling, device_id_type=MESH)
-    pl.semaphore_wait(barrier, len(peers) + 1)
+    pairs = [(lat, rl), (vu, vus.at[core]), (vu2, vus.at[1 - core])]
+    for h, s in order:
+        cs = pl.ds(h * half + s * width, width)
+        pairs += [(wo.at[:, cs], wos.at[core, :, cs]), (wo2.at[:, cs], wos.at[1 - core, :, cs])]
+    loads = [pltpu.make_async_copy(src, dst, in_sems.at[k]) for k, (src, dst) in enumerate(pairs)]
+    for copy in loads:
+        copy.start()
 
     sent = []
 
@@ -406,10 +402,7 @@
         l = rl[:, h * 16 : (h + 1) * 16, :].reshape(256, LATENT)
         ho[:, h * 128 : (h + 1) * 128] = jnp.dot(l, vus[h // 2, h % 2], preferred_element_type=F32).astype(BF16)
 
-    width = half // SUBS
-    wing = width // 2
-
-    def reduce_scatter(turn, fill, bufs, finish):
+    def reduce_scatter(turn, fill, bufs, finish, after=None):
         r1, r2, t1, t2 = bufs
 
         def chunk(h, phase, i, base, size):
@@ -468,9 +461,10 @@
             else:
                 finish(base, width, value)
 
-        order = [(h, s) for s in range(SUBS) for h in range(2)]
-        for h, s in order:
-            fill(h * half + s * width, width)
+        for n, (h, s) in enumerate(order):
+            fill(n, h * half + s * width, width)
+            if turn == 0 and n == 0:
+                pl.semaphore_wait(barrier, len(peers) + 1)
             start(h, s, 0)
         if turn == 0:
             start_weights()
@@ -485,11 +479,13 @@
             middle(h, s, 1)
         for h, s in order:
             total(h, s, 1)
-
-    loads[3].wait()
-    loads[4].wait()
-
-    def fill_out(base, size):
+            if after is not None and h == 1:
+                after(s)
+
+
+    def fill_out(n, base, size):
+        loads[3 + 2 * n].wait()
+        loads[4 + 2 * n].wait()
         cs = pl.ds(base, size)
         v = jnp.dot(ho[:, :256], wos[0, :, cs], preferred_element_type=F32)
         v = v + jnp.dot(ho[:, 256:], wos[1, :, cs], preferred_element_type=F32)
@@ -502,92 +498,106 @@
         m = res[:, cs].astype(F32) + value
         mid[:, cs] = m
         squares.append(jnp.sum(m * m, axis=1, keepdims=True))
-
-    reduce_scatter(0, fill_out, (b1, b2, c1, c2), finish_out)
-    factor = lax.rsqrt(sum(squares) / cols_all + 1e-06)
-    nrm[x, z] = (mid[...] * factor * gain[...]).astype(BF16)
+        nrm[x, z, :, cs] = (m * gain[:, cs]).astype(BF16)
+
+    def block(h, s, i, j, piece):
+        base = h * half + s * width
+        rest = wing + (128 if (h, s) == (1, SUBS - 1) else 0)
+        lo, size = {"all": (0, wing + rest), "low": (0, wing), "high": (wing, rest)}[piece]
+        dx, dz = (j, i) if h == 0 else (i, j)
+        return nrm.at[lax.rem(x + dx + NX, NX), lax.rem(z + dz + NZ, NZ), :, pl.ds(base + lo, size)]
+
+    one, two = {}, {}
+
+    def pass_on(h, s, i, j, piece, k, first, step):
+        ref = block(h, s, i, j, piece)
+        at = (h * SUBS + s) * 20 + k
+        to = device(0, step) if (h == 0) == first else device(step, 0)
+        return send(ref, ref, ag_ss.at[at], ag_rs.at[at], to)
+
+    def spread(h, s, n, i):
+        two[h, s, n] = [pass_on(h, s, i, 0, "all", 4 + 4 * n, False, 1), pass_on(h, s, i, 0, "all", 5 + 4 * n, False, -1)]
+
+    def forward(s, n, i):
+        for h in range(2):
+            got = two[h, s, n]
+            got[0].wait_recv()
+            got.append(pass_on(h, s, i, -1, "low", 6 + 4 * n, False, 1))
+            got[1].wait_recv()
+            got.append(pass_on(h, s, i, 1, "high", 7 + 4 * n, False, -1))
+
+    def gather_start(s):
+        if s == SUBS - 1:
+            scale = lax.rsqrt(sum(squares) / cols_all + 1e-06)
+            rough = scale.astype(BF16).astype(F32)
+            lane = lax.broadcasted_iota(jnp.int32, (16, 128), 1)
+            nrm[x, z, :, cols_all:] = jnp.where(lane < 64, rough, scale - rough).astype(BF16)
+        for h in range(2):
+            one[h, s] = [pass_on(h, s, 0, 0, "all", 0, True, 1), pass_on(h, s, 0, 0, "all", 1, True, -1)]
+        for h in range(2):
+            spread(h, s, 0, 0)
+
+    def gather_next(s):
+        for h in range(2):
+            got = one[h, s]
+            got[0].wait_recv()
+            got.append(pass_on(h, s, -1, 0, "low", 2, True, 1))
+            got[1].wait_recv()
+            got.append(pass_on(h, s, 1, 0, "high", 3, True, -1))
+            spread(h, s, 1, -1)
+            spread(h, s, 2, 1)
+
+    def gather_last(s):
+        for h in range(2):
+            one[h, s][2].wait_recv()
+            one[h, s][3].wait_recv()
+            spread(h, s, 3, 2)
+
+    def gathered(s):
+        for h in range(2):
+            for n in range(4):
+                two[h, s, n][2].wait_recv()
+                two[h, s, n][3].wait_recv()
+
+    def up_step(h, s):
+        cs = pl.ds(h * half + s * width, width)
+        v = lax.dot_general(
+            nrm[:, :, :, cs].reshape(256, width), gus[:, cs], (((1,), (1,)), ((), ())), preferred_element_type=F32
+        )
+        if (h, s) == (0, 0):
+            acc[...] = v
+        else:
+            acc[...] += v
+
+    reduce_scatter(0, fill_out, (b1, b2, c1, c2), finish_out, gather_start)
+    gather_next(0)
+    gather_next(1)
+    forward(0, 0, 0)
+    gather_last(0)
+    forward(1, 0, 0)
+    gather_last(1)
+    forward(0, 1, -1)
+    forward(0, 2, 1)
+    forward(1, 1, -1)
+    forward(0, 3, 2)
+    forward(1, 2, 1)
+    gathered(0)
+    weights_ready(0, 1)
+    up_step(0, 0)
+    forward(1, 3, 2)
+    up_step(1, 0)
+    gathered(1)
+    up_step(0, 1)
+    up_step(1, 1)
+    scales = nrm[:, :, :, cols_all:].reshape(256, 128).astype(F32)
+    scale = scales[:, :1] + scales[:, 64:65]
+    g = acc[:, :640] * scale
+    hid[...] = (g / (1.0 + jnp.exp(-g)) * (acc[:, 640:] * scale)).astype(BF16)
     while sent:
         sent.pop().wait_send()
-
-    quarter = half // 2
-
-    def block(h, i, j, lo, size):
-        cs = pl.ds(h * half + lo, size)
-        dx, dz = (j, i) if h == 0 else (i, j)
-        return nrm.at[lax.rem(x + dx + NX, NX), lax.rem(z + dz + NZ, NZ), :, cs]
-
-    def ag_sems(h, k):
-        return ag_ss.at[h * 20 + k], ag_rs.at[h * 20 + k]
-
-    def along(h, first, i):
-        return device(0, i) if (h == 0) == first else device(i, 0)
-
-    def pass_on(ref, h, k, first, i):
-        return send(ref, ref, *ag_sems(h, k), along(h, first, i))
-
-    one, two = {}, {}
-    for h in range(2):
-        ref = block(h, 0, 0, 0, half)
-        one[h] = [pass_on(ref, h, 0, True, 1), pass_on(ref, h, 1, True, -1)]
-
-    def spread(h, n, i):
-        ref = block(h, i, 0, 0, half)
-        two[h, n] = [pass_on(ref, h, 4 + 4 * n, False, 1), pass_on(ref, h, 5 + 4 * n, False, -1)]
-
-    def forward(h, n, i):
-        two[h, n][0].wait_recv()
-        two[h, n].append(pass_on(block(h, i, -1, 0, quarter), h, 6 + 4 * n, False, 1))
-        two[h, n][1].wait_recv()
-        two[h, n].append(pass_on(block(h, i, 1, quarter, quarter), h, 7 + 4 * n, False, -1))
-
-    for h in range(2):
-        spread(h, 0, 0)
-    for h in range(2):
-        one[h][0].wait_recv()
-        one[h].append(pass_on(block(h, -1, 0, 0, quarter), h, 2, True, 1))
-        one[h][1].wait_recv()
-        one[h].append(pass_on(block(h, 1, 0, quarter, quarter), h, 3, True, -1))
-        spread(h, 1, -1)
-        spread(h, 2, 1)
-    for h in range(2):
-        forward(h, 0, 0)
-    for h in range(2):
-        one[h][2].wait_recv()
-        one[h][3].wait_recv()
-        spread(h, 3, 2)
-    for n, i in ((1, -1), (2, 1), (3, 2)):
-        for h in range(2):
-            forward(h, n, i)
-    for h in range(2):
-        for n in range(4):
-            two[h, n][2].wait_recv()
-            two[h, n][3].wait_recv()
-
-    weights_ready(0, 1)
-    depth = cols_all // 4
-
-    def up_step(k, carry):
-        cs = pl.ds(pl.multiple_of(k * depth, 128), depth)
-        v = lax.dot_general(
-            nrm[:, :, :, cs].reshape(256, depth), gus[:, cs], (((1,), (1,)), ((), ())), preferred_element_type=F32
-        )
-
-        @pl.when(k == 0)
-        def _():
-            acc[...] = v
-
-        @pl.when(k > 0)
-        def _():
-            acc[...] += v
-
-        return carry
-
-    lax.fori_loop(0, 4, up_step, 0)
-    g = acc[:, :640]
-    hid[...] = (g / (1.0 + jnp.exp(-g)) * acc[:, 640:]).astype(BF16)
     weights_ready(2)
 
-    def fill_down(base, size):
+    def fill_down(n, base, size):
         cs = pl.ds(base, size)
         v = jnp.dot(hid[:, : 2 * ff], ds[:, cs], preferred_element_type=F32)
         part[:, :, :, cs] = v.astype(BF16).reshape(NX, NZ, 16, size)
@@ -626,20 +636,20 @@
             pltpu.VMEM((2 * ff, cols), BF16),
             pltpu.VMEM((256, 512), BF16),
             pltpu.VMEM((NX, NZ, 16, cols), BF16),
-            pltpu.VMEM((NX, NZ, 16, cols), BF16),
+            pltpu.VMEM((NX, NZ, 16, cols + 128), BF16),
             pltpu.VMEM((16, cols), F32),
             pltpu.VMEM((256, 1280), F32),
             pltpu.VMEM((256, 640), BF16),
             *rs_bufs,
             *rs_bufs,
-            dma((5,)),
+            dma((3 + 4 * SUBS,)),
             dma((3,)),
             dma((3,)),
             dma((3,)),
             dma((n_rs,)),
             dma((n_rs,)),
-            dma((40,)),
-            dma((40,)),
+            dma((40 * SUBS,)),
+            dma((40 * SUBS,)),
         ],
         compiler_params=pltpu.CompilerParams(collective_id=0, has_side_effects=True, vmem_limit_bytes=VMEM_LIMIT),
         cost_estimate=pl.CostEstimate(flops=12_000_000_000, bytes_accessed=40_000_000, transcendentals=200_000),

time: 171 us -> 168 us (0.982)
  Pallas kernels: 169 us -> 165 us
    pallas_call x1, Pallas kernels: 85.8 us -> 83.4 us  [tail(): pl.pallas_call(tail_kernel, out_shape=jax.ShapeDtypeStruct(residual.shape...]
where the time goes in v5:
time: 168 us; the launch traced here: 167 us
  Pallas kernels  165 us (98%)
    pallas_call x1, Pallas kernels, tail(): pl.pallas_call(tail_kernel, out_shape=jax.ShapeDtypeStruct(residual.shape...  83.4 us
    pallas_call x1, Pallas kernels, attend(): pl.pallas_call(attend_kernel, out_shape=(jax.ShapeDtypeStruct((NX * NZ, r...  81.6 us

profile of v5, /device:TPU:0, one launch (start us, length us, event | category | flops | bytes accessed | tf_op | source)
XLA Modules:
  0.0 167.2 jit_solution(13158098855490384490)
XLA Ops:
  0.7 81.6 %attend.1 = (bf16[16,64,512]{2,1,0:T(8,128)(2,1)}, bf16[2,512,128]{2,1,0:T(8,128)(2,1)}, bf16[256,7168]{1,0:T(8,128)(2,1)}) custom-call(s32[1,768]{1,0:T(1,128)} %bitcast.4, s32[768]{0:T(1024)} %page_of.1, s32[768]{0:T(1024)} %slot_of.1, s32[1]{0:T(128)S(6)} %copy.17.rc, s32[16]{0:T(128)} %lens.1, s32[16,32]{1,0:T(8,128)} %table.1, ...), custom_call_target="tpu_custom_call" | custom-call | tf_op jit(solution)/shard_map/attend/pallas_call | solution.py:287
  82.2 83.4 %tail.1 = bf16[16,7168]{1,0:T(8,128)(2,1)} custom-call(bf16[16,64,512]{2,1,0:T(8,128)(2,1)} %get-tuple-element.8.lat, bf16[2,512,128]{2,1,0:T(8,128)(2,1)} %vu.3, bf16[2,512,128]{2,1,0:T(8,128)(2,1)} %get-tuple-element.9.vu2, bf16[256,7168]{1,0:T(8,128)(2,1)} %wo.3, bf16[256,7168]{1,0:T(8,128)(2,1)} %get-tuple-element.10.wo2, bf16[16,7168]{1,0:T(8,128)(2,1)} %res.1, ...), custom_call_target="tpu_custom_call" | custom-call | flops 12000000000 | bytes 40000000 | tf_op jit(solution)/shard_map/tail/pallas_call | solution.py:626
  165.6 1.6 copy.18

commit v6 on v0

v6 whole, which is shorter than its diff:
```python
import functools

import jax
import jax.numpy as jnp
from jax import lax
from jax.experimental import pallas as pl
from jax.experimental.pallas import tpu as pltpu
from jax.sharding import PartitionSpec as P

LATENT = 512
SOFTMAX_SCALE = 192 ** (-0.5)
LOW = -1e30
MESH = pl.DeviceIdType.MESH
F32 = jnp.float32
BF16 = jnp.bfloat16
VMEM_LIMIT = 60 * 2**20
NX = 4
NZ = 4


def vspec():
    return pl.BlockSpec(memory_space=pltpu.VMEM)


def sspec():
    return pl.BlockSpec(memory_space=pltpu.SMEM)


def aspec():
    return pl.BlockSpec(memory_space=pl.ANY)


SUBS = 2


def layer_kernel(
    src, page_of, slot_of, rc, lens, table, q_hbm, pool_hbm, vu, wo, res, gain, gate, up, down,
    out_ref, gate_2, up_2, down_2,
    via, inbox, rl, nrm, vus, wos, packed, entries_v, entries, b1, b2, c1, c2,
    pool_sems, copy_sems, one_ss, one_rs, two_ss, two_rs, w_ls, w_ss, w_rs, lat_ss, lat_rs, in_sems,
    rs_ss, rs_rs, ag_ss, ag_rs,
):
    me = lax.axis_index("dp")
    core = lax.rem(me, 2)
    chip = me // 2
    x = chip // NZ
    z = lax.rem(chip, NZ)
    rows, heads, width = q_hbm.shape
    count, page, _ = pool_hbm.shape
    part = page // 2
    refs = table.shape[1]
    moves = page_of.shape[0] // (NX * NZ * 2)
    mine = me * moves

    def device(a, b, e):
        return (lax.rem(x + a, NX) * NZ + lax.rem(z + b, NZ)) * 2 + lax.rem(core + e, 2)

    def on(a, b, e):
        return {"dp": device(a, b, e)}

    near = [(0, 0, 1)] + [(a, 0, e) for a in (1, 2, 3) for e in (0, 1)] + [(0, b, e) for b in (1, 2, 3) for e in (0, 1)]
    far = [(a, b, 0) for a in (1, 2, 3) for b in (1, 2, 3)]
    barrier = pltpu.get_barrier_semaphore()
    for at in near + far:
        pl.semaphore_signal(barrier, inc=1, device_id=on(*at), device_id_type=MESH)

    sent = []

    def remote(src, dst, ss, rs, to):
        return pltpu.make_async_remote_copy(
            src_ref=src, dst_ref=dst, send_sem=ss, recv_sem=rs, device_id=to, device_id_type=MESH
        )

    def send(src, dst, ss, rs, to):
        copy = remote(src, dst, ss, rs, to)
        copy.start()
        sent.append(copy)
        return copy

    head_groups = (2, 0, 1, 3)

    def weight_copies():
        refs_of = ((vu, vus.at[core]), (wo, wos.at[core]), (gate, gate_2), (up, up_2), (down, down_2))
        return [remote(one, to, w_ss.at[k], w_rs.at[k], on(0, 0, 1)) for k, (one, to) in enumerate(refs_of)]

    def weight_places():
        return [
            pltpu.make_async_copy(one, to, w_ls.at[k])
            for k, (one, to) in enumerate(((vu, vus.at[core]), (wo, wos.at[core])))
        ]

    def latent_copies(n):
        copies = []
        for b in (2, 1, 3, 0):
            one, to = packed.at[n, lax.rem(z + b, NZ)], rl.at[chip]
            if (head_groups[n], b) == (0, 0):
                copies.append(pltpu.make_async_copy(one, to, pool_sems.at[0]))
            else:
                at = n * 4 + b
                copies.append(remote(one, to, lat_ss.at[at], lat_rs.at[at], on(head_groups[n], b, 0)))
        return copies

    def attention(pool, outbox, pages, mult, acc, top, total, q_ref):
        loads = []
        for k in range(8):
            span = pl.ds(k * (count // 8), count // 8)
            loads.append(pltpu.make_async_copy(pool_hbm.at[span], pool.at[span], pool_sems.at[k]))
        loads.append(pltpu.make_async_copy(q_hbm, q_ref, pool_sems.at[9]))
        for copy in loads:
            copy.start()

        row = lax.broadcasted_iota(jnp.int32, (rows, refs), 0)
        pos = lax.broadcasted_iota(jnp.int32, (rows, refs), 1)
        length = jnp.zeros((rows, refs), jnp.int32)
        for r in range(rows):
            length = jnp.where(row == r, jnp.where(r < rc[0], lens[r], 0), length)
        valid = jnp.clip(length - page * pos, 0, page)
        entry = table[...] * 128 + valid
        for i in range(moves):
            entry = jnp.where(table[...] == slot_of[mine + i], 0, entry)
        entries_v[:, :refs] = entry
        to_scalar = pltpu.make_async_copy(entries_v, entries, pool_sems.at[8])
        to_scalar.start()

        pl.semaphore_wait(barrier, len(near + far))
        for copy in loads:
            copy.wait()

        def pack(i, first):
            d = first + i
            hits = [src[0, d * moves + j] == me for j in range(moves)]
            named = [page_of[d * moves + j] for j in range(moves)]
            early, late = 0, 0
            for j in range(moves):
                late = jnp.where(hits[j], named[j], late)
                early = jnp.where(hits[moves - 1 - j], named[moves - 1 - j], early)
            one, two = pool[early], pool[late]
            rope = jnp.concatenate([one[:, LATENT:], two[:, LATENT:]], axis=1)
            for h in range(2):
                rs = slice(h * part, (h + 1) * part)
                outbox[h, d, :, :LATENT] = one[rs, :LATENT]
                outbox[h, d, :, LATENT : 2 * LATENT] = two[rs, :LATENT]
                outbox[h, d, :, 2 * LATENT :] = rope[rs]
            return first

        one_copies = {}
        final = {}
        local = []

        def deliver(h, a, b, e, src):
            origin = (lax.rem(x + (NX - a if h == 0 else 0), NX) * NZ + lax.rem(z + (0 if h == 0 else NZ - b), NZ)) * 2 + core
            dst = inbox.at[origin, pl.ds(h * part, part), :]
            at = ((a * NZ + b) * 2 + e) * 2 + h
            da, db = (0, b) if h == 0 else (a, 0)
            if (da, db, e) == (0, 0, 0):
                copy = pltpu.make_async_copy(src, dst, copy_sems.at[len(local)])
                copy.start()
                local.append(copy)
            else:
                final[at] = send(src, dst, two_ss.at[at], two_rs.at[at], on(da, db, e))

        for n, a in enumerate((2, 1, 3, 0)):
            xa = lax.rem(x + a, NX)
            lax.fori_loop(0, 8, pack, xa * 8)
            if a:
                one_copies[0, a] = send(
                    outbox.at[0, pl.ds(xa * 8, 8)], via.at[0, a - 1], one_ss.at[a - 1], one_rs.at[a - 1], on(a, 0, 0)
                )
            for b in (2, 1, 3):
                zb = lax.rem(z + b, NZ)
                at = 3 + (b - 1) * 4 + n
                one_copies[1, b, n] = send(
                    outbox.at[1, pl.ds(xa * 8 + zb * 2, 2)],
                    via.at[1, b - 1, pl.ds(xa * 2, 2)],
                    one_ss.at[at],
                    one_rs.at[at],
                    on(0, b, 0),
                )

        def second_hop(k):
            if k:
                one_copies[0, k].wait_recv()
                for n in range(4):
                    one_copies[1, k, n].wait_recv()
            for o in (2, 1, 3, 0):
                for e in range(2):
                    ce = lax.rem(core + e, 2)
                    zo, xo = lax.rem(z + o, NZ), lax.rem(x + o, NX)
                    deliver(0, k, o, e, via.at[0, k - 1, zo * 2 + ce] if k else outbox.at[0, x * 8 + zo * 2 + ce])
                    deliver(1, o, k, e, via.at[1, k - 1, xo * 2 + ce] if k else outbox.at[1, xo * 8 + z * 2 + ce])

        def attend_row(r, carry):
            q = q_ref[r]
            group = 8
            col = lax.broadcasted_iota(jnp.int32, (1, page * group), 1)
            keys, scores = [], []
            for g in range(refs // group):
                es = [entries[r, g * group + i] for i in range(group)]
                k = jnp.concatenate([pool[e >> 7] for e in es], axis=0)
                limit = jnp.zeros((1, page * group), jnp.int32)
                for i, e in enumerate(es):
                    limit = jnp.where((col >> 6) == i, e & 127, limit)
                s = lax.dot_general(q, k, (((1,), (1,)), ((), ())), preferred_element_type=F32) * SOFTMAX_SCALE
                scores.append(jnp.where((col & 63) < limit, s, LOW))
                keys.append(k)
            m = functools.reduce(jnp.maximum, [jnp.max(s, axis=1, keepdims=True) for s in scores])
            t = jnp.zeros((heads, 1), F32)
            o = jnp.zeros((heads, LATENT), F32)
            for s, k in zip(scores, keys):
                p = jnp.exp(s - m)
                t = t + jnp.sum(p, axis=1, keepdims=True)
                o = o + jnp.dot(p.astype(BF16), k[:, :LATENT], preferred_element_type=F32)
            some = m > 0.5 * LOW
            acc[r] = jnp.where(some, o, 0.0)
            top[r] = jnp.broadcast_to(m, (heads, 128))
            total[r] = jnp.broadcast_to(jnp.where(some, t, 0.0), (heads, 128))
            return carry

        for copy in weight_copies() + weight_places():
            copy.start()
        second_hop(0)
        to_scalar.wait()
        lax.fori_loop(0, 5, attend_row, 0)
        second_hop(1)
        second_hop(3)
        lax.fori_loop(5, 9, attend_row, 0)
        second_hop(2)
        lax.fori_loop(9, rows, attend_row, 0)

        block = 16
        whole = (valid == page).astype(F32)
        some = ((valid > 0) & (valid < page)).astype(F32)
        last = jnp.sum(some * valid.astype(F32), axis=1, keepdims=True)
        off = lax.broadcasted_iota(jnp.int32, (rows, page), 1).astype(F32)
        inside = (off < last).astype(F32)
        for i in range(0, moves, 2):
            pair = []
            for j in (i, i + 1):
                hit = (table[...] == slot_of[mine + j]).astype(F32)
                pair.append(
                    jnp.sum(hit * whole, axis=1, keepdims=True) + jnp.sum(hit * some, axis=1, keepdims=True) * inside
                )
            pair = jnp.concatenate(pair, axis=1)
            for r in range(rows):
                mult[r * block : (r + 1) * block, i * page : (i + 2) * page] = jnp.broadcast_to(
                    pair[r : r + 1], (block, 2 * page)
                )

        places = []
        for i in range(moves):
            again = 0
            for j in range(i):
                again = again + (src[0, mine + i] == src[0, mine + j]).astype(jnp.int32)
            places.append((src[0, mine + i], again))

        for copy in local:
            copy.wait()
        for copy in final.values():
            copy.wait_recv()
        while sent:
            sent.pop().wait_send()

        rope = width - LATENT
        for i, (rank, again) in enumerate(places):
            pair = inbox[rank]
            first = again == 0
            here = slice(i * page, (i + 1) * page)
            pages[here, :LATENT] = jnp.where(first, pair[:, :LATENT], pair[:, LATENT : 2 * LATENT])
            pages[here, LATENT:] = jnp.where(
                first, pair[:, 2 * LATENT : 2 * LATENT + rope], pair[:, 2 * LATENT + rope :]
            )

        size = rows * block
        to = lax.broadcasted_iota(jnp.int32, (size, size), 0)
        frm = lax.broadcasted_iota(jnp.int32, (size, size), 1)
        turn = (frm == (to % rows) * block + to // rows).astype(BF16)
        for n, a in enumerate(head_groups):
            xa = lax.rem(x + a, NX)
            hs = pl.ds(pl.multiple_of(xa * block, block), block)
            q = q_ref[:, hs, :].reshape(size, width)
            s = lax.dot_general(q, pages[...], (((1,), (1,)), ((), ())), preferred_element_type=F32) * SOFTMAX_SCALE
            times = mult[...]
            s = jnp.where(times > 0.0, s, LOW)
            old = top[:, hs, :].reshape(size, 128)[:, :1]
            m = jnp.maximum(old, jnp.max(s, axis=1, keepdims=True))
            shrink = jnp.exp(old - m)
            p = jnp.exp(s - m) * times
            t = total[:, hs, :].reshape(size, 128)[:, :1] * shrink + jnp.sum(p, axis=1, keepdims=True)
            o = acc[:, hs, :].reshape(size, LATENT) * shrink
            o = o + jnp.dot(p.astype(BF16), pages[:, :LATENT], preferred_element_type=F32)
            o = (o / jnp.where(t == 0.0, 1.0, t)).astype(BF16)
            o = jnp.dot(turn, o, preferred_element_type=F32).astype(BF16)
            packed[n] = o.reshape(NZ, -1, LATENT)
            for copy in latent_copies(n):
                copy.start()

    def rest(gus, ds, ho, part, mid, acc, hid):
        cols_all = part.shape[3]
        half = cols_all // 2
        ff = gate.shape[0]

        def step_to(dx, dz):
            return on(dx % NX, dz % NZ, 0)

        width = half // SUBS
        wing = width // 2
        order = [(h, s) for s in range(SUBS) for h in range(2)]

        row0 = pl.multiple_of(core * ff, 16)
        row1 = pl.multiple_of(2 * ff - row0 - ff, 16)
        loads = []
        w_copies = weight_copies()
        for k, copy in enumerate(w_copies[2:]):
            copy.wait_recv()
            own, other = ((gate, gate_2), (up, up_2), (down, down_2))[k]
            base = 640 if k == 1 else 0
            into = ds if k == 2 else gus
            loads.append(pltpu.make_async_copy(own, into.at[pl.ds(base + row0, ff), :], in_sems.at[2 * k]))
            loads.append(pltpu.make_async_copy(other, into.at[pl.ds(base + row1, ff), :], in_sems.at[2 * k + 1]))
        for copy in loads:
            copy.start()

        def weights_ready(*ks):
            for k in ks:
                loads[2 * k].wait()
                loads[2 * k + 1].wait()

        for copy in weight_places():
            copy.wait()
        for copy in w_copies[:2]:
            copy.wait_recv()
        sent.extend(w_copies)
        for n in range(4):
            for b, copy in zip((2, 1, 3, 0), latent_copies(n)):
                if (head_groups[n], b) == (0, 0):
                    copy.wait()
                else:
                    copy.wait_recv()
                    sent.append(copy)
        for h in range(4):
            l = rl[:, h * 16 : (h + 1) * 16, :].reshape(256, LATENT)
            ho[:, h * 128 : (h + 1) * 128] = jnp.dot(l, vus[h // 2, h % 2], preferred_element_type=F32).astype(BF16)

        def reduce_scatter(turn, fill, bufs, finish, after=None):
            r1, r2, t1, t2 = bufs

            def chunk(h, phase, i, base, size):
                cs = pl.ds(base, size)
                xi, zi = lax.rem(x + i + NX, NX), lax.rem(z + i + NZ, NZ)
                along_x = (h == 0) == (phase == 0)
                if phase == 0:
                    return part.at[xi, :, :, cs] if along_x else part.at[:, zi, :, cs]
                return part.at[xi, z, :, cs] if along_x else part.at[x, zi, :, cs]

            def to(h, phase, i):
                return step_to(i, 0) if (h == 0) == (phase == 0) else step_to(0, i)

            def sems(h, s, phase, k):
                at = (((turn * 2 + h) * SUBS + s) * 2 + phase) * 6 + k
                return rs_ss.at[at], rs_rs.at[at]

            def bufs_of(h, s, phase):
                first, second = (r1, r2) if phase == 0 else (t1, t2)
                return first.at[h, s], second.at[h, s]

            state = {}

            def start(h, s, phase):
                base = h * half + s * width
                first, second = bufs_of(h, s, phase)
                lo, hi = base, base + wing
                state[h, s, phase] = [
                    send(chunk(h, phase, 2, lo, wing), first.at[0], *sems(h, s, phase, 0), to(h, phase, 1)),
                    send(chunk(h, phase, 2, hi, wing), first.at[1], *sems(h, s, phase, 1), to(h, phase, -1)),
                    send(chunk(h, phase, 1, hi, wing), second.at[0, ..., pl.ds(wing, wing)], *sems(h, s, phase, 2), to(h, phase, 1)),
                    send(chunk(h, phase, -1, lo, wing), second.at[1, ..., pl.ds(0, wing)], *sems(h, s, phase, 3), to(h, phase, -1)),
                ]

            def middle(h, s, phase):
                base = h * half + s * width
                first, second = bufs_of(h, s, phase)
                copies = state[h, s, phase]
                for side, (i, at) in enumerate(((1, 0), (-1, wing))):
                    copies[side].wait_recv()
                    mine = chunk(h, phase, i, base + at, wing)
                    mine[...] = (mine[...].astype(F32) + first[side].astype(F32)).astype(BF16)
                    copies.append(
                        send(mine, second.at[side, ..., pl.ds(at, wing)], *sems(h, s, phase, 4 + side), to(h, phase, i))
                    )

            def total(h, s, phase):
                base = h * half + s * width
                _, second = bufs_of(h, s, phase)
                for copy in state[h, s, phase][2:]:
                    copy.wait_recv()
                mine = chunk(h, phase, 0, base, width)
                value = mine[...].astype(F32) + second[0].astype(F32) + second[1].astype(F32)
                if phase == 0:
                    mine[...] = value.astype(BF16)
                else:
                    finish(base, width, value)

            for n, (h, s) in enumerate(order):
                fill(n, h * half + s * width, width)
                start(h, s, 0)
            if turn == 0:
                gus[pl.ds(2 * ff, 640 - 2 * ff), :] = jnp.zeros((640 - 2 * ff, cols_all), BF16)
                gus[pl.ds(640 + 2 * ff, 640 - 2 * ff), :] = jnp.zeros((640 - 2 * ff, cols_all), BF16)
            for h, s in order:
                middle(h, s, 0)
            for h, s in order:
                total(h, s, 0)
                start(h, s, 1)
            for h, s in order:
                middle(h, s, 1)
            for h, s in order:
                total(h, s, 1)
                if after is not None and h == 1:
                    after(s)


        def fill_out(n, base, size):
            cs = pl.ds(base, size)
            v = jnp.dot(ho[:, :256], wos[0, :, cs], preferred_element_type=F32)
            v = v + jnp.dot(ho[:, 256:], wos[1, :, cs], preferred_element_type=F32)
            part[:, :, :, cs] = v.astype(BF16).reshape(NX, NZ, 16, size)

        squares = []

        def finish_out(base, size, value):
            cs = pl.ds(base, size)
            m = res[:, cs].astype(F32) + value
            mid[:, cs] = m
            squares.append(jnp.sum(m * m, axis=1, keepdims=True))
            nrm[x, z, :, cs] = (m * gain[:, cs]).astype(BF16)

        def block(h, s, i, j, piece):
            base = h * half + s * width
            rest = wing + (128 if (h, s) == (1, SUBS - 1) else 0)
            lo, size = {"all": (0, wing + rest), "low": (0, wing), "high": (wing, rest)}[piece]
            dx, dz = (j, i) if h == 0 else (i, j)
            return nrm.at[lax.rem(x + dx + NX, NX), lax.rem(z + dz + NZ, NZ), :, pl.ds(base + lo, size)]

        one, two = {}, {}

        def pass_on(h, s, i, j, piece, k, first, step):
            ref = block(h, s, i, j, piece)
            at = (h * SUBS + s) * 20 + k
            to = step_to(0, step) if (h == 0) == first else step_to(step, 0)
            return send(ref, ref, ag_ss.at[at], ag_rs.at[at], to)

        def spread(h, s, n, i):
            two[h, s, n] = [pass_on(h, s, i, 0, "all", 4 + 4 * n, False, 1), pass_on(h, s, i, 0, "all", 5 + 4 * n, False, -1)]

        def forward(s, n, i):
            for h in range(2):
                got = two[h, s, n]
                got[0].wait_recv()
                got.append(pass_on(h, s, i, -1, "low", 6 + 4 * n, False, 1))
                got[1].wait_recv()
                got.append(pass_on(h, s, i, 1, "high", 7 + 4 * n, False, -1))

        def gather_start(s):
            if s == SUBS - 1:
                scale = lax.rsqrt(sum(squares) / cols_all + 1e-06)
                rough = scale.astype(BF16).astype(F32)
                lane = lax.broadcasted_iota(jnp.int32, (16, 128), 1)
                nrm[x, z, :, cols_all:] = jnp.where(lane < 64, rough, scale - rough).astype(BF16)
            for h in range(2):
                one[h, s] = [pass_on(h, s, 0, 0, "all", 0, True, 1), pass_on(h, s, 0, 0, "all", 1, True, -1)]
            for h in range(2):
                spread(h, s, 0, 0)

        def gather_next(s):
            for h in range(2):
                got = one[h, s]
                got[0].wait_recv()
                got.append(pass_on(h, s, -1, 0, "low", 2, True, 1))
                got[1].wait_recv()
                got.append(pass_on(h, s, 1, 0, "high", 3, True, -1))
                spread(h, s, 1, -1)
                spread(h, s, 2, 1)

        def gather_last(s):
            for h in range(2):
                one[h, s][2].wait_recv()
                one[h, s][3].wait_recv()
                spread(h, s, 3, 2)

        def gathered(s):
            for h in range(2):
                for n in range(4):
                    two[h, s, n][2].wait_recv()
                    two[h, s, n][3].wait_recv()

        def up_step(h, s):
            cs = pl.ds(h * half + s * width, width)
            v = lax.dot_general(
                nrm[:, :, :, cs].reshape(256, width), gus[:, cs], (((1,), (1,)), ((), ())), preferred_element_type=F32
            )
            if (h, s) == (0, 0):
                acc[...] = v
            else:
                acc[...] += v

        reduce_scatter(0, fill_out, (b1, b2, c1, c2), finish_out, gather_start)
        gather_next(0)
        gather_next(1)
        forward(0, 0, 0)
        gather_last(0)
        forward(1, 0, 0)
        gather_last(1)
        forward(0, 1, -1)
        forward(0, 2, 1)
        forward(1, 1, -1)
        forward(0, 3, 2)
        forward(1, 2, 1)
        gathered(0)
        weights_ready(0, 1)
        up_step(0, 0)
        forward(1, 3, 2)
        up_step(1, 0)
        gathered(1)
        up_step(0, 1)
        up_step(1, 1)
        scales = nrm[:, :, :, cols_all:].reshape(256, 128).astype(F32)
        scale = scales[:, :1] + scales[:, 64:65]
        g = acc[:, :640] * scale
        hid[...] = (g / (1.0 + jnp.exp(-g)) * (acc[:, 640:] * scale)).astype(BF16)
        while sent:
            sent.pop().wait_send()
        weights_ready(2)

        def fill_down(n, base, size):
            cs = pl.ds(base, size)
            v = jnp.dot(hid[:, : 2 * ff], ds[:, cs], preferred_element_type=F32)
            part[:, :, :, cs] = v.astype(BF16).reshape(NX, NZ, 16, size)

        def finish_down(base, size, value):
            cs = pl.ds(base, size)
            out_ref[:, cs] = (mid[:, cs] + value).astype(BF16)

        reduce_scatter(1, fill_down, (b1, b2, c1, c2), finish_down)
        while sent:
            sent.pop().wait_send()


    vmem = pltpu.VMEM
    cols, ff = res.shape[1], gate.shape[0]
    pl.run_scoped(
        attention,
        vmem(pool_hbm.shape, BF16),
        vmem((2, NX * NZ * 2, page // 2, 2 * width), BF16),
        vmem((moves * page, width), BF16),
        vmem((rows * 16, moves * page), F32),
        vmem((rows, heads, LATENT), F32),
        vmem((rows, heads, 128), F32),
        vmem((rows, heads, 128), F32),
        vmem(q_hbm.shape, BF16),
    )
    pl.run_scoped(
        rest,
        vmem((1280, cols), BF16),
        vmem((2 * ff, cols), BF16),
        vmem((256, 512), BF16),
        vmem((NX, NZ, 16, cols), BF16),
        vmem((16, cols), F32),
        vmem((256, 1280), F32),
        vmem((256, 640), BF16),
    )


def layer(src, page_of, slot_of, rc, lens, table, queries, pool, vu, wo, res, gain, gate, up, down):
    rows, heads, width = queries.shape
    page = pool.shape[1]
    ranks = NX * NZ * 2
    cols = res.shape[1]
    block = cols // 2 // SUBS
    n_rs = 2 * 2 * SUBS * 2 * 6
    dma, vmem = pltpu.SemaphoreType.DMA, pltpu.VMEM
    out, _, _, _ = pl.pallas_call(
        layer_kernel,
        out_shape=tuple(jax.ShapeDtypeStruct(a.shape, BF16) for a in (res, gate, up, down)),
        in_specs=[sspec()] * 5 + [vspec()] + [aspec()] * 4 + [vspec()] * 2 + [aspec()] * 3,
        out_specs=(vspec(), aspec(), aspec(), aspec()),
        scratch_shapes=[
            vmem((2, 3, 8, page // 2, 2 * width), BF16),
            vmem((ranks, page, 2 * width), BF16),
            vmem((NX * NZ, rows * heads // (NX * NZ), LATENT), BF16),
            vmem((NX, NZ, 16, cols + 128), BF16),
            vmem((2,) + vu.shape, BF16),
            vmem((2,) + wo.shape, BF16),
            vmem((4, NZ, rows * heads // (NX * NZ), LATENT), BF16),
            vmem((rows, 128), jnp.int32),
            pltpu.SMEM((rows, 128), jnp.int32),
            vmem((2, SUBS, 2, 4, 16, block // 2), BF16),
            vmem((2, SUBS, 2, 4, 16, block), BF16),
            vmem((2, SUBS, 2, 16, block // 2), BF16),
            vmem((2, SUBS, 2, 16, block), BF16),
            dma((10,)),
            dma((8,)),
            dma((15,)),
            dma((15,)),
            dma((64,)),
            dma((64,)),
            dma((2,)),
            dma((5,)),
            dma((5,)),
            dma((16,)),
            dma((16,)),
            dma((6,)),
            dma((n_rs,)),
            dma((n_rs,)),
            dma((40 * SUBS,)),
            dma((40 * SUBS,)),
        ],
        compiler_params=pltpu.CompilerParams(collective_id=0, has_side_effects=True, vmem_limit_bytes=VMEM_LIMIT),
        name="layer",
    )(src, page_of, slot_of, rc, lens, table, queries, pool, vu, wo, res, gain, gate, up, down)
    return out


def body(
    page_pool,
    move_source,
    move_page,
    move_slot,
    row_count,
    lengths,
    page_table,
    queries,
    value_up,
    out_proj,
    residual,
    norm_gain,
    gate_proj,
    up_proj,
    down_proj,
):
    return layer(
        move_source.reshape(1, -1), move_page, move_slot, row_count, lengths, page_table, queries, page_pool,
        value_up, out_proj, residual, norm_gain.reshape(1, -1), gate_proj.T, up_proj.T, down_proj,
    )


def solution(mesh):
    in_specs = (
        P(("rep", "dp"), None, None),
        P("rep", None),
        P("rep"),
        P("rep"),
        P(("rep", "dp")),
        P(("rep", "dp")),
        P(("rep", "dp"), None),
        P(("rep", "dp"), None, None),
        P("dp", None, None),
        P("dp", None),
        P(("rep", "dp"), None),
        P(),
        P(None, "dp"),
        P(None, "dp"),
        P("dp", None),
    )
    out_specs = P(("rep", "dp"), None)
    return jax.shard_map(body, mesh=mesh, in_specs=in_specs, out_specs=out_specs, check_vma=False)
```

time: 552 us -> 165 us (0.30)
  waiting for transfers between devices: 289 us -> 0 us
  Pallas kernels: 0 us -> 163 us
  local copies, waits for them, and re-layouts: 109 us -> 1.64 us
  matrix products: 70.5 us -> 0 us
  other arithmetic: 31.5 us -> 0 us
  blocking collectives: 26.2 us -> 0 us
  between operations: 14 us -> 0.66 us
  starting transfers between devices: 8.8 us -> 0 us
    reduce_scatter x2 -> x0, waiting for transfers between devices: 174 us -> none  [the longest x1 87.8 us: body(): lax.psum_scatter(jnp.dot(rows_slice, down_proj, preferred_element_type=jn...]
    pallas_call x0 -> x1, Pallas kernels: none -> 163 us  [layer(): pl.pallas_call(layer_kernel, out_shape=tuple((jax.ShapeDtypeStruct(a.shap...]
    gather x18 -> x0, local copies, waits for them, and re-layouts: 84.5 us -> none  [the longest x16 74 us: one_row(): tokens = cache_pages[table_row].reshape(-1, cache_pages.shape[2])]
    dot_general x37 -> x0, matrix products: 70.5 us -> none  [the longest x16 30.7 us: one_row(): jnp.einsum('hk,tk->ht', query_row, tokens, preferred_element_type=jnp.flo...]
    all_to_all x1 -> x0, waiting for transfers between devices: 64.1 us -> none  [body(): lax.all_to_all(outgoing, 'dp', split_axis=0, concat_axis=0, tiled=True)]
    all_gather x1 -> x0, waiting for transfers between devices: 50.2 us -> none  [body(): row_piece = lax.all_gather(normed, 'dp', axis=0, tiled=True)]
    all_to_all x1 -> x0, blocking collectives: 26.2 us -> none  [body(): lax.all_to_all(latent_out, 'dp', split_axis=1, concat_axis=0, tiled=True)]
    select_n x19 -> x0, other arithmetic: 13.1 us -> none  [the longest x16 11.1 us: one_row(): tokens = cache_pages[table_row].reshape(-1, cache_pages.shape[2])]
  transfers between devices with their start and end apart: 4 -> 0, of which waited for: 4 -> 0; matrix products, arithmetic and copies ran while one was open for 0% -> 0% of each run, Pallas kernels for 0% -> 0%
where the time goes in v6:
time: 165 us
  Pallas kernels  163 us (99%)
    pallas_call x1, Pallas kernels, layer(): pl.pallas_call(layer_kernel, out_shape=tuple((jax.ShapeDtypeStruct(a.shap...  163 us

profile of v6, /device:TPU:0, one launch (start us, length us, event | category | flops | bytes accessed | tf_op | source)
XLA Modules:
  0.0 165.1 jit_solution(8751457994979358874)
XLA Ops:
  0.7 162.8 %layer.1 = (bf16[16,7168]{1,0:T(8,128)(2,1)}, bf16[288,7168]{1,0:T(8,128)(2,1)}, bf16[288,7168]{1,0:T(8,128)(2,1)}, bf16[288,7168]{1,0:T(8,128)(2,1)}) custom-call(s32[1,768]{1,0:T(1,128)} %bitcast.7, s32[768]{0:T(1024)} %page_of.1, s32[768]{0:T(1024)} %slot_of.1, s32[1]{0:T(128)S(6)} %copy.17.rc, s32[16]{0:T(128)} %lens.1, s32[16,32]{1,0:T(8,128)} %table.1, ...), custom_call_target="tpu_custom_call" | custom-call | tf_op jit(solution)/shard_map/layer/pallas_call | solution.py:581
  163.5 1.6 copy.18

commit v7 on v6

--- a/solution.py
+++ b/solution.py
@@ -105,7 +105,6 @@
         for k in range(8):
             span = pl.ds(k * (count // 8), count // 8)
             loads.append(pltpu.make_async_copy(pool_hbm.at[span], pool.at[span], pool_sems.at[k]))
-        loads.append(pltpu.make_async_copy(q_hbm, q_ref, pool_sems.at[9]))
         for copy in loads:
             copy.start()
 
@@ -218,8 +217,11 @@
 
         for copy in weight_copies() + weight_places():
             copy.start()
+        load_q = pltpu.make_async_copy(q_hbm, q_ref, pool_sems.at[9])
+        load_q.start()
         second_hop(0)
         to_scalar.wait()
+        load_q.wait()
         lax.fori_loop(0, 5, attend_row, 0)
         second_hop(1)
         second_hop(3)
@@ -317,9 +319,6 @@
             into = ds if k == 2 else gus
             loads.append(pltpu.make_async_copy(own, into.at[pl.ds(base + row0, ff), :], in_sems.at[2 * k]))
             loads.append(pltpu.make_async_copy(other, into.at[pl.ds(base + row1, ff), :], in_sems.at[2 * k + 1]))
-        for copy in loads:
-            copy.start()
-
         def weights_ready(*ks):
             for k in ks:
                 loads[2 * k].wait()
@@ -365,16 +364,20 @@
 
             state = {}
 
-            def start(h, s, phase):
-                base = h * half + s * width
+            def start(h, s, phase, side):
+                base = h * half + s * width + side * wing
                 first, second = bufs_of(h, s, phase)
-                lo, hi = base, base + wing
-                state[h, s, phase] = [
-                    send(chunk(h, phase, 2, lo, wing), first.at[0], *sems(h, s, phase, 0), to(h, phase, 1)),
-                    send(chunk(h, phase, 2, hi, wing), first.at[1], *sems(h, s, phase, 1), to(h, phase, -1)),
-                    send(chunk(h, phase, 1, hi, wing), second.at[0, ..., pl.ds(wing, wing)], *sems(h, s, phase, 2), to(h, phase, 1)),
-                    send(chunk(h, phase, -1, lo, wing), second.at[1, ..., pl.ds(0, wing)], *sems(h, s, phase, 3), to(h, phase, -1)),
-                ]
+                step = 1 - 2 * side
+                copies = state.setdefault((h, s, phase), {})
+                copies[side] = send(
+                    chunk(h, phase, 2, base, wing), first.at[side], *sems(h, s, phase, side), to(h, phase, step)
+                )
+                copies[3 - side] = send(
+                    chunk(h, phase, -step, base, wing),
+                    second.at[1 - side, ..., pl.ds(side * wing, wing)],
+                    *sems(h, s, phase, 3 - side),
+                    to(h, phase, -step),
+                )
 
             def middle(h, s, phase):
                 base = h * half + s * width
@@ -384,15 +387,15 @@
                     copies[side].wait_recv()
                     mine = chunk(h, phase, i, base + at, wing)
                     mine[...] = (mine[...].astype(F32) + first[side].astype(F32)).astype(BF16)
-                    copies.append(
-                        send(mine, second.at[side, ..., pl.ds(at, wing)], *sems(h, s, phase, 4 + side), to(h, phase, i))
+                    copies[4 + side] = send(
+                        mine, second.at[side, ..., pl.ds(at, wing)], *sems(h, s, phase, 4 + side), to(h, phase, i)
                     )
 
             def total(h, s, phase):
                 base = h * half + s * width
                 _, second = bufs_of(h, s, phase)
-                for copy in state[h, s, phase][2:]:
-                    copy.wait_recv()
+                for k in range(2, 6):
+                    state[h, s, phase][k].wait_recv()
                 mine = chunk(h, phase, 0, base, width)
                 value = mine[...].astype(F32) + second[0].astype(F32) + second[1].astype(F32)
                 if phase == 0:
@@ -400,17 +403,23 @@
                 else:
                     finish(base, width, value)
 
-            for n, (h, s) in enumerate(order):
-                fill(n, h * half + s * width, width)
-                start(h, s, 0)
+            for s in range(SUBS):
+                for side in range(2):
+                    for h in range(2):
+                        fill(h * half + s * width + side * wing, wing)
+                        start(h, s, 0, side)
             if turn == 0:
                 gus[pl.ds(2 * ff, 640 - 2 * ff), :] = jnp.zeros((640 - 2 * ff, cols_all), BF16)
                 gus[pl.ds(640 + 2 * ff, 640 - 2 * ff), :] = jnp.zeros((640 - 2 * ff, cols_all), BF16)
             for h, s in order:
                 middle(h, s, 0)
+            if turn == 0:
+                for copy in loads[:4]:
+                    copy.start()
             for h, s in order:
                 total(h, s, 0)
-                start(h, s, 1)
+                start(h, s, 1, 0)
+                start(h, s, 1, 1)
             for h, s in order:
                 middle(h, s, 1)
             for h, s in order:
@@ -419,7 +428,7 @@
                     after(s)
 
 
-        def fill_out(n, base, size):
+        def fill_out(base, size):
             cs = pl.ds(base, size)
             v = jnp.dot(ho[:, :256], wos[0, :, cs], preferred_element_type=F32)
             v = v + jnp.dot(ho[:, 256:], wos[1, :, cs], preferred_element_type=F32)
@@ -510,15 +519,17 @@
         gather_last(0)
         forward(1, 0, 0)
         gather_last(1)
+        for copy in loads[4:]:
+            copy.start()
         forward(0, 1, -1)
         forward(0, 2, 1)
         forward(1, 1, -1)
         forward(0, 3, 2)
         forward(1, 2, 1)
+        forward(1, 3, 2)
         gathered(0)
         weights_ready(0, 1)
         up_step(0, 0)
-        forward(1, 3, 2)
         up_step(1, 0)
         gathered(1)
         up_step(0, 1)
@@ -531,7 +542,7 @@
             sent.pop().wait_send()
         weights_ready(2)
 
-        def fill_down(n, base, size):
+        def fill_down(base, size):
             cs = pl.ds(base, size)
             v = jnp.dot(hid[:, : 2 * ff], ds[:, cs], preferred_element_type=F32)
             part[:, :, :, cs] = v.astype(BF16).reshape(NX, NZ, 16, size)

time: 165 us -> 163 us (0.988)
  Pallas kernels: 163 us -> 160 us
    pallas_call x1, Pallas kernels: 163 us -> 160 us  [layer(): pl.pallas_call(layer_kernel, out_shape=tuple((jax.ShapeDtypeStruct(a.shap...]
where the time goes in v7:
time: 163 us; the launch traced here: 162 us
  Pallas kernels  160 us (98%)
  local copies, waits for them, and re-layouts  1.64 us (1%)
    pallas_call x1, Pallas kernels, layer(): pl.pallas_call(layer_kernel, out_shape=tuple((jax.ShapeDtypeStruct(a.shap...  160 us

profile of v7, /device:TPU:0, one launch (start us, length us, event | category | flops | bytes accessed | tf_op | source)
XLA Modules:
  0.0 162.2 jit_solution(9888646624218217897)
XLA Ops:
  0.7 159.8 %layer.1 = (bf16[16,7168]{1,0:T(8,128)(2,1)}, bf16[288,7168]{1,0:T(8,128)(2,1)}, bf16[288,7168]{1,0:T(8,128)(2,1)}, bf16[288,7168]{1,0:T(8,128)(2,1)}) custom-call(s32[1,768]{1,0:T(1,128)} %bitcast.7, s32[768]{0:T(1024)} %page_of.1, s32[768]{0:T(1024)} %slot_of.1, s32[1]{0:T(128)S(6)} %copy.17.rc, s32[16]{0:T(128)} %lens.1, s32[16,32]{1,0:T(8,128)} %table.1, ...), custom_call_target="tpu_custom_call" | custom-call | tf_op jit(solution)/shard_map/layer/pallas_call | solution.py:592
  160.5 1.6 %copy.18 = bf16[16,7168]{1,0:T(8,128)(2,1)} copy(bf16[16,7168]{1,0:T(8,128)(2,1)} %get-tuple-element.6) | data formatting | bytes 458752

commit v8 on v7

--- a/solution.py
+++ b/solution.py
@@ -496,11 +496,10 @@
                 one[h, s][3].wait_recv()
                 spread(h, s, 3, 2)
 
-        def gathered(s):
-            for h in range(2):
-                for n in range(4):
-                    two[h, s, n][2].wait_recv()
-                    two[h, s, n][3].wait_recv()
+        def gathered(h, s):
+            for n in range(4):
+                two[h, s, n][2].wait_recv()
+                two[h, s, n][3].wait_recv()
 
         def up_step(h, s):
             cs = pl.ds(h * half + s * width, width)
@@ -527,13 +526,11 @@
         forward(0, 3, 2)
         forward(1, 2, 1)
         forward(1, 3, 2)
-        gathered(0)
         weights_ready(0, 1)
-        up_step(0, 0)
-        up_step(1, 0)
-        gathered(1)
-        up_step(0, 1)
-        up_step(1, 1)
+        for s in range(SUBS):
+            for h in range(2):
+                gathered(h, s)
+                up_step(h, s)
         scales = nrm[:, :, :, cols_all:].reshape(256, 128).astype(F32)
         scale = scales[:, :1] + scales[:, 64:65]
         g = acc[:, :640] * scale

time: 163 us -> 162 us (level)
  no operation moved by 1% of the time
where the time goes in v8:
time: 162 us
  Pallas kernels  160 us (99%)
  local copies, waits for them, and re-layouts  1.64 us (1%)
    pallas_call x1, Pallas kernels, layer(): pl.pallas_call(layer_kernel, out_shape=tuple((jax.ShapeDtypeStruct(a.shap...  160 us

profile of v8, /device:TPU:0, one launch (start us, length us, event | category | flops | bytes accessed | tf_op | source)
XLA Modules:
  0.0 162.0 jit_solution(8201122847973218477)
XLA Ops:
  0.7 159.7 %layer.1 = (bf16[16,7168]{1,0:T(8,128)(2,1)}, bf16[288,7168]{1,0:T(8,128)(2,1)}, bf16[288,7168]{1,0:T(8,128)(2,1)}, bf16[288,7168]{1,0:T(8,128)(2,1)}) custom-call(s32[1,768]{1,0:T(1,128)} %bitcast.7, s32[768]{0:T(1024)} %page_of.1, s32[768]{0:T(1024)} %slot_of.1, s32[1]{0:T(128)S(6)} %copy.17.rc, s32[16]{0:T(128)} %lens.1, s32[16,32]{1,0:T(8,128)} %table.1, ...), custom_call_target="tpu_custom_call" | custom-call | tf_op jit(solution)/shard_map/layer/pallas_call | solution.py:589
  160.4 1.6 %copy.18 = bf16[16,7168]{1,0:T(8,128)(2,1)} copy(bf16[16,7168]{1,0:T(8,128)(2,1)} %get-tuple-element.6) | data formatting | bytes 458752
